TPU v7x, 32 devices: a whole 2x2x4 slice. The times are simulated.
32 devices in a mesh: seq: 8 (over z, core), ctx: 4 (over y, x).
Axes of the slice: x: 2, y: 2, z: 4, core: 2. Of those that a mesh axis runs over, the one named last changes fastest.
Arguments:
- features: bfloat16 [8, 2048, 2560], P('seq', 'ctx'), may hold values from -6 to 6
- step_sizes: float32 [8, 40, 2048], P('seq', None, 'ctx'), may hold values from 0 to 1, as said below
- rate_logs: float32 [40], replicated, may hold values from -8 to 3
- input_map: bfloat16 [8, 2048, 128], P('seq', 'ctx'), may hold values from -0.5 to 0.5
- output_map: bfloat16 [8, 2048, 128], P('seq', 'ctx'), may hold values from -6 to 6
- skip_gain: float32 [40], replicated, may hold values from 0.5 to 1.5
- state_first: bfloat16 [8, 40, 64, 128], P('seq'), may hold values from -0.5 to 0.5
- upstream: bfloat16 [8, 2048, 2560], P('seq', 'ctx'), may hold values from -45 to 45
- state_last: bfloat16 [8, 40, 64, 128], P('seq'), may hold values from -768 to 768
Outputs:
- grad_features: bfloat16 [8, 2048, 2560], P('seq', 'ctx')
- grad_steps: float32 [8, 40, 2048], P('seq', None, 'ctx')
- grad_input_map: float32 [8, 2048, 128], P('seq', 'ctx')
- grad_output_map: float32 [8, 2048, 128], P('seq', 'ctx')
- grad_rate_logs: float32 [40], replicated
- grad_skip_gain: float32 [40], replicated
Inputs may be any that keep to these rules, and one draw needn't show every extreme that they name: `step_sizes`: Positive.
All inputs are finite; a program needn't handle non-finite values.
Results may differ from a plain program's by a relative error of at most 0.0055.
Values sent between devices are 32-bit elements; how exact they have to be, the bound alone decides.
A program may use at most 192 MiB of HBM per device.

v0:
```python
from functools import partial

import jax
import jax.numpy as jnp
from jax import lax
from jax.sharding import PartitionSpec as P

Q = 256


def partner(value, axis, distance):
    return lax.ppermute(value, axis, [(i, i ^ 1 << distance) for i in range(lax.axis_size(axis))])


def split_blocks(features, step_sizes, input_map, output_map, upstream, head_count):
    length = features.shape[0]
    blocks = length // Q
    head_size = features.shape[1] // head_count
    return (
        features.reshape(blocks, Q, head_count, head_size),
        jnp.transpose(step_sizes.reshape(head_count, blocks, Q), (1, 0, 2)),
        input_map.reshape(blocks, Q, -1),
        output_map.reshape(blocks, Q, -1),
        upstream.reshape(blocks, Q, head_count, head_size),
    )


def block_local(block_data, decay_rates):
    inputs, steps, map_in, map_out, upstream = block_data
    log_sums = jnp.cumsum(steps * decay_rates[:, None], axis=1)
    end_logs = log_sums[:, Q - 1]
    scaled = jnp.exp(end_logs[:, None] - log_sums) * steps
    decayed_in = (inputs.astype(jnp.float32) * jnp.transpose(scaled)[:, :, None]).astype(
        jnp.bfloat16
    )
    decayed_up = (
        upstream.astype(jnp.float32) * jnp.exp(jnp.transpose(log_sums))[:, :, None]
    ).astype(jnp.bfloat16)
    fresh_block = jnp.einsum("shp,sn->hpn", decayed_in, map_in, preferred_element_type=jnp.float32)
    readout = jnp.einsum("thp,tn->hpn", decayed_up, map_out, preferred_element_type=jnp.float32)
    scores = jnp.dot(map_out, map_in.T, preferred_element_type=jnp.float32)
    inner_dots = jnp.einsum("thp,shp->hts", upstream, inputs, preferred_element_type=jnp.float32)
    causal = jnp.arange(Q)[:, None] >= jnp.arange(Q)[None, :]
    spread = jnp.minimum(log_sums[:, :, None] - log_sums[:, None, :], 0.0)
    kernel = jnp.where(causal[None], jnp.exp(spread), 0.0) * scores[None]
    mixing = (kernel * steps[:, None, :]).astype(jnp.bfloat16)
    grad_inputs = jnp.einsum("hts,thp->shp", mixing, upstream, preferred_element_type=jnp.float32)
    weighted = kernel * inner_dots
    pulled = weighted * steps[:, None, :]
    score_grads = jnp.sum(pulled, axis=0).astype(jnp.bfloat16)
    grad_in = jnp.dot(score_grads.T, map_out, preferred_element_type=jnp.float32)
    grad_out = jnp.dot(score_grads, map_in, preferred_element_type=jnp.float32)
    log_grads = jnp.sum(pulled, axis=2) - jnp.sum(pulled, axis=1)
    step_grads = jnp.sum(weighted, axis=1)
    skip_part = jnp.sum(jnp.diagonal(inner_dots, axis1=1, axis2=2), axis=1)
    return (
        log_sums,
        scaled,
        decayed_in,
        decayed_up,
        fresh_block,
        readout,
        grad_inputs,
        grad_in,
        grad_out,
        log_grads,
        step_grads,
        skip_part,
    )


def enter_block(running, element):
    end_log, fresh_block = element
    return (jnp.exp(end_log)[:, None, None] * running + fresh_block, running)


def finish_block(block_data, decay_rates, skip_gain):
    (
        inputs,
        steps,
        map_in,
        map_out,
        upstream,
        log_sums,
        scaled,
        decayed_in,
        decayed_up,
        entering,
        leaving,
        grad_inputs,
        grad_in,
        grad_out,
        log_grads,
        step_grads,
    ) = block_data
    end_logs = log_sums[:, Q - 1]
    entering_half = entering.astype(jnp.bfloat16)
    leaving_half = leaving.astype(jnp.bfloat16)
    carried_out = jnp.einsum(
        "tn,hpn->thp", map_out, entering_half, preferred_element_type=jnp.float32
    )
    carried_in = jnp.einsum("sn,hpn->shp", map_in, leaving_half, preferred_element_type=jnp.float32)
    upstream_wide = upstream.astype(jnp.float32)
    readout_dots = jnp.transpose(jnp.sum(upstream_wide * carried_out, axis=2))
    input_dots = jnp.transpose(jnp.sum(inputs.astype(jnp.float32) * carried_in, axis=2))
    scaled_rows = jnp.transpose(scaled)[:, :, None]
    features_grad = (
        grad_inputs + scaled_rows * carried_in + skip_gain[None, :, None] * upstream_wide
    )
    in_grad = grad_in + jnp.einsum(
        "shp,hpn->sn", decayed_in, leaving_half, preferred_element_type=jnp.float32
    )
    out_grad = grad_out + jnp.einsum(
        "thp,hpn->tn", decayed_up, entering_half, preferred_element_type=jnp.float32
    )
    fresh_terms = scaled * input_dots
    end_extra = jnp.sum(fresh_terms, axis=1) + jnp.exp(end_logs) * jnp.sum(
        leaving * entering, axis=(1, 2)
    )
    last_token = (jnp.arange(Q) == Q - 1).astype(jnp.float32)
    total_logs = (
        log_grads
        + jnp.exp(log_sums) * readout_dots
        - fresh_terms
        + end_extra[:, None] * last_token[None, :]
    )
    through = jnp.flip(jnp.cumsum(jnp.flip(total_logs, 1), axis=1), 1)
    steps_grad = (
        decay_rates[:, None] * through
        + step_grads
        + jnp.exp(end_logs[:, None] - log_sums) * input_dots
    )
    rate_part = jnp.sum(steps * through, axis=1)
    return (features_grad, steps_grad, in_grad, out_grad, rate_part)


def region_finish(stacked, local_parts, decay_rates, skip_gain, state_in, cot_out):
    end_logs = local_parts[0][:, :, Q - 1]
    _, entering = lax.scan(enter_block, state_in, (end_logs, local_parts[4]))
    _, leaving = lax.scan(enter_block, cot_out, (end_logs, local_parts[5]), reverse=True)
    block_data = stacked + local_parts[:4] + (entering, leaving) + local_parts[6:11]
    return lax.map(partial(finish_block, decay_rates=decay_rates, skip_gain=skip_gain), block_data)


def assemble(finished, local_parts, length, head_count):
    features_grad = finished[0].reshape(length, -1)
    steps_grad = jnp.transpose(finished[1], (1, 0, 2)).reshape(head_count, length)
    in_grad = finished[2].reshape(length, -1)
    out_grad = finished[3].reshape(length, -1)
    rate_sum = jnp.sum(finished[4], axis=0)
    skip_sum = jnp.sum(local_parts[11], axis=0)
    return (features_grad, steps_grad, in_grad, out_grad, rate_sum, skip_sum)


def compose(earlier, later):
    return (earlier[0] * later[0], later[0][:, None, None] * earlier[1] + later[1])


def select_pair(flag, option_true, option_false):
    return tuple(
        (
            jnp.where(flag, first_item, second_item)
            for first_item, second_item in zip(option_true, option_false)
        )
    )


def local(
    features,
    step_sizes,
    rate_logs,
    input_map,
    output_map,
    skip_gain,
    state_first,
    upstream,
    state_last,
):
    head_count = rate_logs.shape[0]
    length = features.shape[1]
    decay_rates = -jnp.exp(rate_logs)
    stacked = split_blocks(
        features[0], step_sizes[0], input_map[0], output_map[0], upstream[0], head_count
    )
    local_parts = lax.map(partial(block_local, decay_rates=decay_rates), stacked)
    end_logs = local_parts[0][:, :, Q - 1]
    zero_state = jnp.zeros_like(local_parts[4][0])
    block_state, _ = lax.scan(enter_block, zero_state, (end_logs, local_parts[4]))
    block_cotangent, _ = lax.scan(enter_block, zero_state, (end_logs, local_parts[5]), reverse=True)
    block_decay = jnp.exp(jnp.sum(end_logs, axis=0))
    unit_decay = jnp.ones_like(block_decay)
    position = lax.axis_index("ctx")
    forward_total = (block_decay, block_state)
    forward_prefix = (unit_decay, zero_state)
    backward_total = (block_decay, block_cotangent)
    backward_suffix = (unit_decay, zero_state)
    for bit_level in range(lax.axis_size("ctx").bit_length() - 1):
        received = partner(
            (forward_total[0], forward_total[1], backward_total[0], backward_total[1]),
            "ctx",
            bit_level,
        )
        peer_forward = (received[0], received[1])
        peer_backward = (received[2], received[3])
        is_upper = (position >> bit_level) % 2 == 1
        forward_prefix = select_pair(
            is_upper, compose(peer_forward, forward_prefix), forward_prefix
        )
        forward_total = select_pair(
            is_upper, compose(peer_forward, forward_total), compose(forward_total, peer_forward)
        )
        backward_suffix = select_pair(
            is_upper, backward_suffix, compose(peer_backward, backward_suffix)
        )
        backward_total = select_pair(
            is_upper, compose(backward_total, peer_backward), compose(peer_backward, backward_total)
        )
    prefix_decay, prefix_state = forward_prefix
    suffix_decay, suffix_cotangent = backward_suffix
    state_in = prefix_state + prefix_decay[:, None, None] * state_first[0].astype(jnp.float32)
    cot_out = suffix_cotangent + suffix_decay[:, None, None] * state_last[0].astype(jnp.float32)
    finished = region_finish(stacked, local_parts, decay_rates, skip_gain, state_in, cot_out)
    grads = assemble(finished, local_parts, length, head_count)
    within_rates, within_skip = lax.psum((grads[4], grads[5]), "ctx")
    total_rates, total_skip = lax.psum((within_rates, within_skip), "seq")
    return (
        grads[0].astype(jnp.bfloat16)[None],
        grads[1][None],
        grads[2][None],
        grads[3][None],
        decay_rates * total_rates,
        total_skip,
    )


def solution(mesh):
    return jax.shard_map(
        local,
        mesh=mesh,
        in_specs=(
            P("seq", "ctx", None),
            P("seq", None, "ctx"),
            P(),
            P("seq", "ctx", None),
            P("seq", "ctx", None),
            P(),
            P("seq", None, None, None),
            P("seq", "ctx", None),
            P("seq", None, None, None),
        ),
        out_specs=(
            P("seq", "ctx", None),
            P("seq", None, "ctx"),
            P("seq", "ctx", None),
            P("seq", "ctx", None),
            P(),
            P(),
        ),
        check_vma=False,
    )
```

profile of v0, /device:TPU:0, one launch (start us, length us, event | category | flops | bytes accessed | tf_op | source)
XLA Modules:
  0.0 366.7 jit_solution(6456302413714950321)
XLA Ops:
  0.7 7.6 %reshape.251 = bf16[2,256,40,64]{3,2,1,0:T(8,128)(2,1)} reshape(bf16[1,512,2560]{2,1,0:T(8,128)(2,1)} %param.21) | data formatting | bytes 5242880 | tf_op jit(solution)/shard_map/reshape;squeeze | solution.py:20
  8.3 6.5 %copy.137 = bf16[2,256,40,64]{1,3,2,0:T(8,128)(2,1)} copy(bf16[2,256,40,64]{3,2,1,0:T(8,128)(2,1)} %reshape.251) | data formatting | bytes 5242880 | tf_op jit(solution)/shard_map/while | solution.py:185
  14.8 4.4 %reshape.252 = bf16[2,256,40,64]{3,2,1,0:T(8,128)(2,1)} reshape(bf16[1,512,2560]{2,1,0:T(8,128)(2,1)S(1)} %copy-done.9) | data formatting | bytes 5242880 | tf_op jit(solution)/shard_map/reshape;squeeze | solution.py:24
  19.2 5.2 %copy.138 = bf16[2,256,40,64]{1,3,2,0:T(8,128)(2,1)S(1)} copy(bf16[2,256,40,64]{3,2,1,0:T(8,128)(2,1)} %reshape.252) | data formatting | bytes 5242880 | tf_op jit(solution)/shard_map/while | solution.py:185
  30.2 101.7 %while.110 = (s32[]{:T(128)}, f32[2,40,256]{2,1,0:T(8,128)S(1)}, f32[2,40,256]{2,1,0:T(8,128)S(1)}, bf16[2,256,40,64]{1,3,2,0:T(8,128)(2,1)}, bf16[2,256,40,64]{...) while((s32[]{:T(128)}, f32[2,40,256]{2,1,0:T(8,128)S(1)}, ...), condition=%wide.region_8.9_spmd.clone, body=%wide.region_0.8_spmd.sunk.clone | while | flops 1108145280 | bytes 127566464 | solution.py:185
  33.5 9.3 %multiply_reduce_fusion.8 = (f32[40,256]{1,0:T(8,128)}, f32[40,256]{1,0:T(8,128)}, bf16[256,256]{1,0:T(8,128)(2,1)S(1)}, f32[40,256]{1,0:T(8,128)}, f32[40,256,256]{2,1,0:T(8,128)}) fusion(f32[40,256]{1,0:T(8,128)S(1)} %get-tuple-element.1415, f32[256,256]{1,0:T(8,128)S(1)} %fusion.204, f32[40,256]{1,0:T(8,128)S(1)} %copy_bitcast_fusion.6, ...), kind=kOutput, calls=%fused_computation.81.clone.1.clone | convolution fusion | flops 361662464 | bytes 13812736 | tf_op jit(solution)/shard_map/while/body/eval_jaxpr/thp,shp->hts/dot_general | solution.py:42
  42.8 20.7 %copy.213 = f32[40,256,256]{0,2,1:T(8,128)} copy(f32[40,256,256]{2,1,0:T(8,128)} %get-tuple-element.1422) | data formatting | bytes 20971520 | tf_op jit(solution)/shard_map/while/body/eval_jaxpr/thp,shp->hts/dot_general | solution.py:42
  63.5 2.3 gather_fusion
  69.1 6.1 %bitcast_dynamic-update-slice_fusion.16 = f32[2,256,40,64]{1,3,2,0:T(8,128)} fusion(f32[2,256,40,64]{1,3,2,0:T(8,128)} %get-tuple-element.1577, s32[]{:T(128)} %get-tuple-element.1570, f32[40,256]{1,0:T(8,128)} %copy-done.11, f32[256,256]{1,0:T(8,128)S(1)} %fusion.204, f32[40,256]{1,0:T(8,128)S(1)} %copy_bitcast_fusion.6, ...), kind=kOutput, calls=%fused_computation.91.clone.1.clone | convolution fusion | flops 351272960 | bytes 4383744 | tf_op jit(solution)/shard_map/while/body/eval_jaxpr/hts,thp->shp/dot_general | solution.py:47
  84.4 9.3 %multiply_reduce_fusion.8 = (f32[40,256]{1,0:T(8,128)}, f32[40,256]{1,0:T(8,128)}, bf16[256,256]{1,0:T(8,128)(2,1)S(1)}, f32[40,256]{1,0:T(8,128)}, f32[40,256,256]{2,1,0:T(8,128)}) fusion(f32[40,256]{1,0:T(8,128)S(1)} %get-tuple-element.1415, f32[256,256]{1,0:T(8,128)S(1)} %fusion.204, f32[40,256]{1,0:T(8,128)S(1)} %copy_bitcast_fusion.6, ...), kind=kOutput, calls=%fused_computation.81.clone.1.clone | convolution fusion | flops 361662464 | bytes 13812736 | tf_op jit(solution)/shard_map/while/body/eval_jaxpr/thp,shp->hts/dot_general | solution.py:42
  93.8 20.7 %copy.213 = f32[40,256,256]{0,2,1:T(8,128)} copy(f32[40,256,256]{2,1,0:T(8,128)} %get-tuple-element.1422) | data formatting | bytes 20971520 | tf_op jit(solution)/shard_map/while/body/eval_jaxpr/thp,shp->hts/dot_general | solution.py:42
  114.5 2.3 gather_fusion
  120.0 6.1 %bitcast_dynamic-update-slice_fusion.16 = f32[2,256,40,64]{1,3,2,0:T(8,128)} fusion(f32[2,256,40,64]{1,3,2,0:T(8,128)} %get-tuple-element.1577, s32[]{:T(128)} %get-tuple-element.1570, f32[40,256]{1,0:T(8,128)} %copy-done.11, f32[256,256]{1,0:T(8,128)S(1)} %fusion.204, f32[40,256]{1,0:T(8,128)S(1)} %copy_bitcast_fusion.6, ...), kind=kOutput, calls=%fused_computation.91.clone.1.clone | convolution fusion | flops 351272960 | bytes 4383744 | tf_op jit(solution)/shard_map/while/body/eval_jaxpr/hts,thp->shp/dot_general | solution.py:47
  132.2 5.6 %while.114 = (s32[]{:T(128)}, f32[40,64,128]{2,1,0:T(8,128)}, f32[2,40]{1,0:T(2,128)S(1)}, f32[2,40,64,128]{3,2,1,0:T(8,128)}) while((s32[]{:T(128)}, f32[40,64,128]{2,1,0:T(8,128)}, f32[2,40]{1,0:T(2,128)S(1)}, f32[2,40,64,128]{3,2,1,0:T(8,128)}) %tuple.214), condition=%wide.region_15.16_spmd.clone.clone, body=%wide.region_14.15_spmd.clone.sunk.clone | while | flops 983044 | bytes 3932723 | solution.py:189
  132.2 2.6 bitcast_add_fusion.16
  134.8 3.0 bitcast_add_fusion.16
  137.8 2.9 collective-permute-start
  140.8 5.6 %while.115 = (s32[]{:T(128)}, f32[40,64,128]{2,1,0:T(8,128)}, f32[2,40]{1,0:T(2,128)S(1)}, f32[2,40,64,128]{3,2,1,0:T(8,128)}) while((s32[]{:T(128)}, f32[40,64,128]{2,1,0:T(8,128)}, f32[2,40]{1,0:T(2,128)S(1)}, f32[2,40,64,128]{3,2,1,0:T(8,128)}) %tuple.235), condition=%wide.region_11.12_spmd.clone.clone, body=%wide.region_10.11_spmd.clone.sunk.clone | while | flops 983043 | bytes 3932711 | solution.py:188
  140.8 2.6 bitcast_add_fusion.17
  143.4 3.0 bitcast_add_fusion.17
  148.4 49.6 %collective-permute-done.1 = f32[40]{0:T(128)S(1)} collective-permute-done((f32[40]{0:T(128)S(1)}, f32[40]{0:T(128)S(1)}, u32[]{:S(2)}, u32[]{:S(2)}) %collective-permute-start.1) | collective-permute-done | bytes 192 | tf_op jit(solution)/shard_map/ppermute | solution.py:12
  197.9 4.6 %add_select_fusion.2 = (f32[40,64,128]{2,1,0:T(8,128)}, f32[40,64,128]{2,1,0:T(8,128)}) fusion(f32[40,64,128]{2,1,0:T(8,128)} %collective-permute-done.4, f32[40,64,128]{2,1,0:T(8,128)} %get-tuple-element.484, f32[40]{0:T(128)S(1)} %exp.94, f32[40]{0:T(128)S(1)} %collective-permute-done.1, pred[]{:T(512)S(6)} %eq.17, f32[40,64,128]{2,1,0:T(8,128)} %get-tuple-element.480, ...), kind=kLoop, calls=%fused_computation.159 | loop fusion | flops 3276800 | bytes 7864641 | tf_op jit(solution)/shard_map/jit(_where)/select_n | solution.py:162
  206.9 25.9 %collective-permute-done.3 = f32[40]{0:T(128)S(1)} collective-permute-done((f32[40]{0:T(128)S(1)}, f32[40]{0:T(128)S(1)}, u32[]{:S(2)}, u32[]{:S(2)}) %collective-permute-start.3) | collective-permute-done | bytes 192 | tf_op jit(solution)/shard_map/ppermute | solution.py:12
  234.3 3.0 fusion.111
  239.1 10.8 %while.112 = (s32[]{:T(128)}, f32[40,64,128]{2,1,0:T(8,128)}, f32[2,40,64,128]{3,2,1,0:T(8,128)}, f32[2,40]{1,0:T(2,128)S(1)}, f32[2,40,64,128]{3,2,1,0:T(8,128)}) while((s32[]{:T(128)}, f32[40,64,128]{2,1,0:T(8,128)}, f32[2,40,64,128]{3,2,1,0:T(8,128)}, f32[2,40]{1,0:T(2,128)S(1)}, f32[2,40,64,128]{3,2,1,0:T(8,128)}) %tuple.236), condition=%wide.region_13.14_spmd.clone, body=%wide.region_12.13_spmd.sunk.clone | while | flops 655362 | bytes 17040448 | solution.py:139
  239.1 2.7 bitcast_dynamic-update-slice_fusion.19
  241.8 2.7 bitcast_add_fusion.15
  244.5 2.7 bitcast_dynamic-update-slice_fusion.19
  247.2 2.7 bitcast_add_fusion.15
  249.9 12.2 %collective-permute-done.2 = f32[40,64,128]{2,1,0:T(8,128)} collective-permute-done((f32[40,64,128]{2,1,0:T(8,128)}, f32[40,64,128]{2,1,0:T(8,128)}, u32[]{:S(2)}, u32[]{:S(2)}) %collective-permute-start.2) | collective-permute-done | bytes 1310752 | tf_op jit(solution)/shard_map/ppermute | solution.py:12
  262.1 3.3 fusion.110
  267.3 11.1 %while.111 = (s32[]{:T(128)}, f32[40,64,128]{2,1,0:T(8,128)}, f32[2,40,64,128]{3,2,1,0:T(8,128)}, f32[2,40]{1,0:T(2,128)S(1)}, f32[2,40,64,128]{3,2,1,0:T(8,128)}) while((s32[]{:T(128)}, f32[40,64,128]{2,1,0:T(8,128)}, f32[2,40,64,128]{3,2,1,0:T(8,128)}, f32[2,40]{1,0:T(2,128)S(1)}, f32[2,40,64,128]{3,2,1,0:T(8,128)}) %tuple.237), condition=%wide.region_17.18_spmd.clone, body=%wide.region_16.17_spmd.sunk.clone | while | flops 655363 | bytes 6554165 | solution.py:140
  267.3 2.6 bitcast_dynamic-update-slice_fusion.18
  269.9 3.0 bitcast_add_fusion.14
  272.9 2.5 bitcast_dynamic-update-slice_fusion.18
  275.4 3.0 bitcast_add_fusion.14
  280.4 46.2 %while.113 = (s32[]{:T(128)}, bf16[2,256,40,64]{1,3,2,0:T(8,128)(2,1)}, f32[2,40,256]{1,2,0:T(8,128)}, f32[2,256,128]{2,1,0:T(8,128)}, f32[2,256,128]{2,1,0:T(8,...) while((s32[]{:T(128)}, ...), condition=%wide.region_26.27_spmd.clone, body=%wide.region_18.26_spmd.sunk.clone | while | flops 680462912 | bytes 38098744 | solution.py:142
  281.8 4.0 %fusion.215 = (bf16[2,256,40,64]{1,3,2,0:T(8,128)(2,1)}, f32[256,40,64]{0,2,1:T(8,128)S(1)}) fusion(bf16[2,256,40,64]{1,3,2,0:T(8,128)(2,1)} %get-tuple-element.1687, s32[]{:T(128)} %get-tuple-element.1686, f32[2,256,40,64]{1,3,2,0:T(8,128)} %get-tuple-element.1716, f32[40]{0:T(128)S(1)} %get-tuple-element.1720, f32[256,40]{0,1:T(8,128)S(1)} %bitcast.491, ...), kind=kOutput, calls=%fused_computation.21.clone.1.clone | convolution fusion | flops 171048960 | bytes 9938944 | tf_op jit(solution)/shard_map/while/body/eval_jaxpr/sn,hpn->shp/dot_general | solution.py:102
  286.6 2.1 multiply_reduce_fusion.9
  297.7 2.9 fusion.220
  300.6 2.9 fusion.221
  304.9 4.0 %fusion.215 = (bf16[2,256,40,64]{1,3,2,0:T(8,128)(2,1)}, f32[256,40,64]{0,2,1:T(8,128)S(1)}) fusion(bf16[2,256,40,64]{1,3,2,0:T(8,128)(2,1)} %get-tuple-element.1687, s32[]{:T(128)} %get-tuple-element.1686, f32[2,256,40,64]{1,3,2,0:T(8,128)} %get-tuple-element.1716, f32[40]{0:T(128)S(1)} %get-tuple-element.1720, f32[256,40]{0,1:T(8,128)S(1)} %bitcast.491, ...), kind=kOutput, calls=%fused_computation.21.clone.1.clone | convolution fusion | flops 171048960 | bytes 9938944 | tf_op jit(solution)/shard_map/while/body/eval_jaxpr/sn,hpn->shp/dot_general | solution.py:102
  320.8 2.9 fusion.220
  323.7 2.9 fusion.221
  327.3 9.1 %all-reduce.1 = (f32[40]{0:T(128)S(1)}, f32[40]{0:T(128)S(1)}) all-reduce(f32[40]{0:T(128)S(1)} %reduce_sum.122, f32[40]{0:T(128)} %reduce_sum.123), channel_id=1, replica_groups=mesh['seq'=8,'ctx'=4] {'ctx'}, use_global_device_ids=true, to_apply=%region_28.29 | all-reduce | flops 80 | bytes 640 | tf_op jit(solution)/shard_map/psum | solution.py:224
  336.4 14.1 %all-reduce = (f32[40]{0:T(128)S(1)}, f32[40]{0:T(128)}) all-reduce(f32[40]{0:T(128)S(1)} %get-tuple-element.945, f32[40]{0:T(128)S(1)} %get-tuple-element.946), channel_id=1, replica_groups=mesh['seq'=8,'ctx'=4] {'seq'}, use_global_device_ids=true, to_apply=%region_29.30 | all-reduce | flops 80 | bytes 640 | tf_op jit(solution)/shard_map/psum | solution.py:225
  351.7 6.5 %copy.150 = bf16[2,256,40,64]{3,2,1,0:T(8,128)(2,1)} copy(bf16[2,256,40,64]{1,3,2,0:T(8,128)(2,1)} %get-tuple-element.491) | data formatting | bytes 5242880
  358.1 7.8 %reshape.250 = bf16[1,512,2560]{2,1,0:T(8,128)(2,1)} reshape(bf16[2,256,40,64]{3,2,1,0:T(8,128)(2,1)} %copy.150) | data formatting | bytes 5242880
  (252 shorter events, 70.9 us)
Async XLA Ops:
  8.3 6.5 %copy-start.9 = (bf16[1,512,2560]{2,1,0:T(8,128)(2,1)S(1)}, bf16[1,512,2560]{2,1,0:T(8,128)(2,1)}, u32[]{:S(2)}) copy-start(bf16[1,512,2560]{2,1,0:T(8,128)(2,1)} %param.28) | copy-start | bytes 7864324
  19.2 5.2 %copy-start.21 = (f32[1,40,512]{2,1,0:T(8,128)S(1)}, f32[1,40,512]{2,1,0:T(8,128)}, u32[]{:S(2)}) copy-start(f32[1,40,512]{2,1,0:T(8,128)} %param.22) | copy-start | bytes 245764
  19.2 5.9 %copy-start.27 = (f32[40]{0:T(128)S(1)}, f32[40]{0:T(128)}, u32[]{:S(2)}) copy-start(f32[40]{0:T(128)} %param.23) | copy-start | bytes 484
  25.1 5.1 %copy-start.5 = (bf16[1,512,128]{2,1,0:T(8,128)(2,1)S(1)}, bf16[1,512,128]{2,1,0:T(8,128)(2,1)}, u32[]{:S(2)}) copy-start(bf16[1,512,128]{2,1,0:T(8,128)(2,1)} %param.24) | copy-start | bytes 393220
  25.1 5.1 %copy-start.6 = (bf16[1,512,128]{2,1,0:T(8,128)(2,1)S(1)}, bf16[1,512,128]{2,1,0:T(8,128)(2,1)}, u32[]{:S(2)}) copy-start(bf16[1,512,128]{2,1,0:T(8,128)(2,1)} %param.25) | copy-start | bytes 393220
  32.6 10.2 %copy-start.11 = (f32[40,256]{1,0:T(8,128)}, f32[40,256]{1,0:T(8,128)S(1)}, u32[]{:S(2)}) copy-start(f32[40,256]{1,0:T(8,128)S(1)} %get-tuple-element.1415) | copy-start | bytes 122884 | tf_op jit(solution)/shard_map/while
  33.5 9.4 %copy-start.10 = (pred[256,256]{1,0:T(8,128)(4,1)}, pred[256,256]{1,0:T(8,128)(4,1)S(1)}, u32[]{:S(2)}) copy-start(pred[256,256]{1,0:T(8,128)(4,1)S(1)} %iota_compare_fusion.3) | copy-start | bytes 196612 | tf_op jit(solution)/shard_map/while
  69.1 6.2 %copy-start = (bf16[2,256,40,64]{1,3,2,0:T(8,128)(2,1)S(1)}, bf16[2,256,40,64]{1,3,2,0:T(8,128)(2,1)}, u32[]{:S(2)}) copy-start(bf16[2,256,40,64]{1,3,2,0:T(8,128)(2,1)} %get-tuple-element.1604) | copy-start | bytes 7864324 | tf_op jit(solution)/shard_map/while
  69.1 6.2 %copy-start.23 = (bf16[2,256,40,64]{1,3,2,0:T(8,128)(2,1)S(1)}, bf16[2,256,40,64]{1,3,2,0:T(8,128)(2,1)}, u32[]{:S(2)}) copy-start(bf16[2,256,40,64]{1,3,2,0:T(8,128)(2,1)} %get-tuple-element.1573) | copy-start | bytes 7864324 | tf_op jit(solution)/shard_map/while
  69.1 6.2 %copy-start.25 = (bf16[2,256,40,64]{1,3,2,0:T(8,128)(2,1)S(1)}, bf16[2,256,40,64]{1,3,2,0:T(8,128)(2,1)}, u32[]{:S(2)}) copy-start(bf16[2,256,40,64]{1,3,2,0:T(8,128)(2,1)} %get-tuple-element.1574) | copy-start | bytes 7864324 | tf_op jit(solution)/shard_map/while
  75.3 1.7 copy-start.2
  76.4 4.8 %copy-start.24 = (bf16[2,256,40,64]{1,3,2,0:T(8,128)(2,1)}, bf16[2,256,40,64]{1,3,2,0:T(8,128)(2,1)S(1)}, u32[]{:S(2)}) copy-start(bf16[2,256,40,64]{1,3,2,0:T(8,128)(2,1)S(1)} %get-tuple-element.1592) | copy-start | bytes 7864324 | tf_op jit(solution)/shard_map/while
  76.4 4.8 %copy-start.26 = (bf16[2,256,40,64]{1,3,2,0:T(8,128)(2,1)}, bf16[2,256,40,64]{1,3,2,0:T(8,128)(2,1)S(1)}, u32[]{:S(2)}) copy-start(bf16[2,256,40,64]{1,3,2,0:T(8,128)(2,1)S(1)} %get-tuple-element.1593) | copy-start | bytes 7864324 | tf_op jit(solution)/shard_map/while
  77.0 4.1 %copy-start.13 = (f32[2,40,256]{2,1,0:T(8,128)S(1)}, f32[2,40,256]{2,1,0:T(8,128)}, u32[]{:S(2)}) copy-start(f32[2,40,256]{2,1,0:T(8,128)} %copy-done.12) | copy-start | bytes 245764 | tf_op jit(solution)/shard_map/while
  77.0 4.1 %copy-start.17 = (f32[2,40,256]{2,1,0:T(8,128)S(1)}, f32[2,40,256]{2,1,0:T(8,128)}, u32[]{:S(2)}) copy-start(f32[2,40,256]{2,1,0:T(8,128)} %copy-done.16) | copy-start | bytes 245764 | tf_op jit(solution)/shard_map/while
  77.6 1.9 copy-start.3
  83.6 10.2 %copy-start.11 = (f32[40,256]{1,0:T(8,128)}, f32[40,256]{1,0:T(8,128)S(1)}, u32[]{:S(2)}) copy-start(f32[40,256]{1,0:T(8,128)S(1)} %get-tuple-element.1415) | copy-start | bytes 122884 | tf_op jit(solution)/shard_map/while
  84.4 9.4 %copy-start.10 = (pred[256,256]{1,0:T(8,128)(4,1)}, pred[256,256]{1,0:T(8,128)(4,1)S(1)}, u32[]{:S(2)}) copy-start(pred[256,256]{1,0:T(8,128)(4,1)S(1)} %iota_compare_fusion.3) | copy-start | bytes 196612 | tf_op jit(solution)/shard_map/while
  120.0 6.2 %copy-start = (bf16[2,256,40,64]{1,3,2,0:T(8,128)(2,1)S(1)}, bf16[2,256,40,64]{1,3,2,0:T(8,128)(2,1)}, u32[]{:S(2)}) copy-start(bf16[2,256,40,64]{1,3,2,0:T(8,128)(2,1)} %get-tuple-element.1604) | copy-start | bytes 7864324 | tf_op jit(solution)/shard_map/while
  120.0 6.2 %copy-start.23 = (bf16[2,256,40,64]{1,3,2,0:T(8,128)(2,1)S(1)}, bf16[2,256,40,64]{1,3,2,0:T(8,128)(2,1)}, u32[]{:S(2)}) copy-start(bf16[2,256,40,64]{1,3,2,0:T(8,128)(2,1)} %get-tuple-element.1573) | copy-start | bytes 7864324 | tf_op jit(solution)/shard_map/while
  120.0 6.2 %copy-start.25 = (bf16[2,256,40,64]{1,3,2,0:T(8,128)(2,1)S(1)}, bf16[2,256,40,64]{1,3,2,0:T(8,128)(2,1)}, u32[]{:S(2)}) copy-start(bf16[2,256,40,64]{1,3,2,0:T(8,128)(2,1)} %get-tuple-element.1574) | copy-start | bytes 7864324 | tf_op jit(solution)/shard_map/while
  127.3 4.7 %copy-start.24 = (bf16[2,256,40,64]{1,3,2,0:T(8,128)(2,1)}, bf16[2,256,40,64]{1,3,2,0:T(8,128)(2,1)S(1)}, u32[]{:S(2)}) copy-start(bf16[2,256,40,64]{1,3,2,0:T(8,128)(2,1)S(1)} %get-tuple-element.1592) | copy-start | bytes 7864324 | tf_op jit(solution)/shard_map/while
  127.3 4.7 %copy-start.26 = (bf16[2,256,40,64]{1,3,2,0:T(8,128)(2,1)}, bf16[2,256,40,64]{1,3,2,0:T(8,128)(2,1)S(1)}, u32[]{:S(2)}) copy-start(bf16[2,256,40,64]{1,3,2,0:T(8,128)(2,1)S(1)} %get-tuple-element.1593) | copy-start | bytes 7864324 | tf_op jit(solution)/shard_map/while
  128.0 4.0 %copy-start.13 = (f32[2,40,256]{2,1,0:T(8,128)S(1)}, f32[2,40,256]{2,1,0:T(8,128)}, u32[]{:S(2)}) copy-start(f32[2,40,256]{2,1,0:T(8,128)} %copy-done.12) | copy-start | bytes 245764 | tf_op jit(solution)/shard_map/while
  128.0 4.0 %copy-start.17 = (f32[2,40,256]{2,1,0:T(8,128)S(1)}, f32[2,40,256]{2,1,0:T(8,128)}, u32[]{:S(2)}) copy-start(f32[2,40,256]{2,1,0:T(8,128)} %copy-done.16) | copy-start | bytes 245764 | tf_op jit(solution)/shard_map/while
  128.5 1.9 copy-start.3
  137.8 60.1 %collective-permute-start = (f32[40,64,128]{2,1,0:T(8,128)}, f32[40,64,128]{2,1,0:T(8,128)}, u32[]{:S(2)}, u32[]{:S(2)}) collective-permute-start(f32[40,64,128]{2,1,0:T(8,128)} %get-tuple-element.480), channel_id=1, source_target_pairs={{0,1},{1,0},{2,3},{3,2},{4,5},{5,4},{6,7},{7,6},{8,9},{9,8},{10,11... | collective-permute-start | bytes 3932168 | tf_op jit(solution)/shard_map/ppermute | solution.py:12
  146.3 51.6 %collective-permute-start.4 = (f32[40,64,128]{2,1,0:T(8,128)}, f32[40,64,128]{2,1,0:T(8,128)}, u32[]{:S(2)}, u32[]{:S(2)}) collective-permute-start(f32[40,64,128]{2,1,0:T(8,128)} %get-tuple-element.484), channel_id=1, source_target_pairs={{0,1},{1,0},{2,3},{3,2},{4,5},{5,4},{6,7},{7,6},{8,9},{9,8},{10,11... | collective-permute-start | bytes 3932168 | tf_op jit(solution)/shard_map/ppermute | solution.py:12
  146.3 51.6 %collective-permute-start.1 = (f32[40]{0:T(128)S(1)}, f32[40]{0:T(128)S(1)}, u32[]{:S(2)}, u32[]{:S(2)}) collective-permute-start(f32[40]{0:T(128)S(1)} %exp.94), channel_id=1, source_target_pairs={{0,1},{1,0},{2,3},{3,2},{4,5},{5,4},{6,7},{7,6},{8,9},{9,8},{10,11... | collective-permute-start | bytes 488 | tf_op jit(solution)/shard_map/ppermute | solution.py:12
  202.5 31.7 %collective-permute-start.5 = (f32[40,64,128]{2,1,0:T(8,128)}, f32[40,64,128]{2,1,0:T(8,128)}, u32[]{:S(2)}, u32[]{:S(2)}) collective-permute-start(f32[40,64,128]{2,1,0:T(8,128)} %get-tuple-element.971), channel_id=1, source_target_pairs={{0,2},{1,3},{2,0},{3,1},{4,6},{5,7},{6,4},{7,5},{8,10},{9,11},{10,... | collective-permute-start | bytes 3932168 | tf_op jit(solution)/shard_map/ppermute | solution.py:12
  206.1 26.7 %collective-permute-start.3 = (f32[40]{0:T(128)S(1)}, f32[40]{0:T(128)S(1)}, u32[]{:S(2)}, u32[]{:S(2)}) collective-permute-start(f32[40]{0:T(128)S(1)} %exponential_multiply_fusion), channel_id=1, source_target_pairs={{0,2},{1,3},{2,0},{3,1},{4,6},{5,7},{6,4},{7,5},{8,10},{9,11},{10,... | collective-permute-start | bytes 488 | tf_op jit(solution)/shard_map/ppermute | solution.py:12
  232.8 29.3 %collective-permute-start.2 = (f32[40,64,128]{2,1,0:T(8,128)}, f32[40,64,128]{2,1,0:T(8,128)}, u32[]{:S(2)}, u32[]{:S(2)}) collective-permute-start(f32[40,64,128]{2,1,0:T(8,128)} %get-tuple-element.972), channel_id=1, source_target_pairs={{0,2},{1,3},{2,0},{3,1},{4,6},{5,7},{6,4},{7,5},{8,10},{9,11},{10,... | collective-permute-start | bytes 3932168 | tf_op jit(solution)/shard_map/ppermute | solution.py:12
  239.1 2.7 copy-start.4
  244.5 2.7 copy-start.4
  267.3 13.1 %copy-start.22 = (f32[40]{0:T(128)S(1)}, f32[40]{0:T(128)}, u32[]{:S(2)}) copy-start(f32[40]{0:T(128)} %param.26) | copy-start | bytes 484
  280.4 8.3 %copy-start.18 = (f32[2,40,256]{2,1,0:T(8,128)}, f32[2,40,256]{2,1,0:T(8,128)S(1)}, u32[]{:S(2)}) copy-start(f32[2,40,256]{2,1,0:T(8,128)S(1)} %get-tuple-element.1717) | copy-start | bytes 245764 | tf_op jit(solution)/shard_map/while
  280.4 9.8 %copy-start.7 = (bf16[2,256,128]{2,1,0:T(8,128)(2,1)}, bf16[2,256,128]{2,1,0:T(8,128)(2,1)S(1)}, u32[]{:S(2)}) copy-start(bf16[2,256,128]{2,1,0:T(8,128)(2,1)S(1)} %get-tuple-element.1725) | copy-start | bytes 393220 | tf_op jit(solution)/shard_map/while
  281.8 4.0 %copy-start.1 = (bf16[2,256,40,64]{1,3,2,0:T(8,128)(2,1)S(1)}, bf16[2,256,40,64]{1,3,2,0:T(8,128)(2,1)}, u32[]{:S(2)}) copy-start(bf16[2,256,40,64]{1,3,2,0:T(8,128)(2,1)} %get-tuple-element.1727) | copy-start | bytes 7864324 | tf_op jit(solution)/shard_map/while
  296.3 7.2 %copy-start.8 = (bf16[2,256,128]{2,1,0:T(8,128)(2,1)S(1)}, bf16[2,256,128]{2,1,0:T(8,128)(2,1)}, u32[]{:S(2)}) copy-start(bf16[2,256,128]{2,1,0:T(8,128)(2,1)} %copy-done.7) | copy-start | bytes 393220 | tf_op jit(solution)/shard_map/while
  296.3 7.2 %copy-start.15 = (f32[2,40,256]{2,1,0:T(8,128)S(1)}, f32[2,40,256]{2,1,0:T(8,128)}, u32[]{:S(2)}) copy-start(f32[2,40,256]{2,1,0:T(8,128)} %copy-done.14) | copy-start | bytes 245764 | tf_op jit(solution)/shard_map/while
  296.3 7.2 %copy-start.19 = (f32[2,40,256]{2,1,0:T(8,128)S(1)}, f32[2,40,256]{2,1,0:T(8,128)}, u32[]{:S(2)}) copy-start(f32[2,40,256]{2,1,0:T(8,128)} %copy-done.18) | copy-start | bytes 245764 | tf_op jit(solution)/shard_map/while
  303.5 8.3 %copy-start.18 = (f32[2,40,256]{2,1,0:T(8,128)}, f32[2,40,256]{2,1,0:T(8,128)S(1)}, u32[]{:S(2)}) copy-start(f32[2,40,256]{2,1,0:T(8,128)S(1)} %get-tuple-element.1717) | copy-start | bytes 245764 | tf_op jit(solution)/shard_map/while
  303.5 9.8 %copy-start.7 = (bf16[2,256,128]{2,1,0:T(8,128)(2,1)}, bf16[2,256,128]{2,1,0:T(8,128)(2,1)S(1)}, u32[]{:S(2)}) copy-start(bf16[2,256,128]{2,1,0:T(8,128)(2,1)S(1)} %get-tuple-element.1725) | copy-start | bytes 393220 | tf_op jit(solution)/shard_map/while
  304.9 4.0 %copy-start.1 = (bf16[2,256,40,64]{1,3,2,0:T(8,128)(2,1)S(1)}, bf16[2,256,40,64]{1,3,2,0:T(8,128)(2,1)}, u32[]{:S(2)}) copy-start(bf16[2,256,40,64]{1,3,2,0:T(8,128)(2,1)} %get-tuple-element.1727) | copy-start | bytes 7864324 | tf_op jit(solution)/shard_map/while
  319.4 7.2 %copy-start.8 = (bf16[2,256,128]{2,1,0:T(8,128)(2,1)S(1)}, bf16[2,256,128]{2,1,0:T(8,128)(2,1)}, u32[]{:S(2)}) copy-start(bf16[2,256,128]{2,1,0:T(8,128)(2,1)} %copy-done.7) | copy-start | bytes 393220 | tf_op jit(solution)/shard_map/while
  319.4 7.2 %copy-start.15 = (f32[2,40,256]{2,1,0:T(8,128)S(1)}, f32[2,40,256]{2,1,0:T(8,128)}, u32[]{:S(2)}) copy-start(f32[2,40,256]{2,1,0:T(8,128)} %copy-done.14) | copy-start | bytes 245764 | tf_op jit(solution)/shard_map/while
  319.4 7.2 %copy-start.19 = (f32[2,40,256]{2,1,0:T(8,128)S(1)}, f32[2,40,256]{2,1,0:T(8,128)}, u32[]{:S(2)}) copy-start(f32[2,40,256]{2,1,0:T(8,128)} %copy-done.18) | copy-start | bytes 245764 | tf_op jit(solution)/shard_map/while
  358.1 7.8 %copy-start.20 = (f32[2,40,256]{1,2,0:T(8,128)S(1)}, f32[2,40,256]{1,2,0:T(8,128)}, u32[]{:S(2)}) copy-start(f32[2,40,256]{1,2,0:T(8,128)} %get-tuple-element.492) | copy-start | bytes 245764
  (7 other events, 5.9 us)
where the time goes:
time: 370 us; the launch traced here: 367 us
  local copies, waits for them, and re-layouts  130 us (35%)
  waiting for transfers between devices  87.7 us (24%)
  matrix products  62.1 us (17%)
  other arithmetic  53.7 us (15%)
  blocking collectives  23.2 us (6%)
  starting transfers between devices  8.45 us (2%)
    ppermute x6, waiting for transfers between devices, partner(): lax.ppermute(value, axis, [(i, i ^ 1 << distance) for i in range(lax.axis...  87.7 us
    dot_general x2, local copies, waits for them, and re-layouts, block_local(): jnp.einsum('thp,shp->hts', upstream, inputs, preferred_element_type=jnp.f...  41.4 us
    add x8, other arithmetic, enter_block(): return (jnp.exp(end_log)[:, None, None] * running + fresh_block, running)  22.5 us
    dot_general x2, matrix products, block_local(): jnp.einsum('thp,shp->hts', upstream, inputs, preferred_element_type=jnp.f...  18.7 us
    unnamed x16, local copies, waits for them, and re-layouts  14.3 us
    psum x1, blocking collectives, local(): total_rates, total_skip = lax.psum((within_rates, within_skip), 'seq')  14.1 us
    dynamic_update_slice x8, local copies, waits for them, and re-layouts, local(): lax.map(partial(block_local, decay_rates=decay_rates), stacked)  13.2 us
    dot_general x2, matrix products, block_local(): jnp.einsum('hts,thp->shp', mixing, upstream, preferred_element_type=jnp.f...  12.2 us
  transfers between devices with their start and end apart: 6, of which 3 were waited for; matrix products, arithmetic and copies ran while one was open for 6% of the time, Pallas kernels for 0%

commit v1 on v0

v1 whole, which is shorter than its diff:
```python
from functools import partial

import jax
import jax.numpy as jnp
from jax import lax
from jax.experimental import pallas as pl
from jax.experimental.pallas import tpu as pltpu
from jax.sharding import PartitionSpec as P

Q = 256
G = 8
LOG2E = 1.4426950408889634
F32 = jnp.float32
BF16 = jnp.bfloat16
NT = (((1,), (1,)), ((), ()))
TN = (((0,), (0,)), ((), ()))


def fdot(a, b):
    return jnp.dot(a, b, preferred_element_type=F32)


def exact_dot(a, b):
    return jnp.dot(a, b, preferred_element_type=F32, precision=lax.Precision.HIGHEST)


def tri(kind):
    row = lax.broadcasted_iota(jnp.int32, (Q, Q), 0)
    col = lax.broadcasted_iota(jnp.int32, (Q, Q), 1)
    return (row <= col if kind == "prefix" else row >= col).astype(F32)


def states_kernel(size, flags, steps, rates, x, g, bmap, cmap, *outs):
    fresh_out, read_out, ls_out, esum_out, xt_out, gt_out = outs[:6]
    payloads = outs[6:]
    blocks = steps.shape[1] // Q
    prefix = tri("prefix")
    fresh, read, ends = [], [], []
    for c in range(blocks):
        cols = slice(c * Q, (c + 1) * Q)
        step = steps[:, cols]
        logs = exact_dot(step * rates[...], prefix)
        ls_out[:, cols] = logs
        end = logs[:, Q - 1 :]
        scaled = jnp.exp(end - logs) * step
        grown = jnp.exp(logs)
        xt = x[cols, :].T
        gt = g[cols, :].T
        xt_out[:, cols] = xt
        gt_out[:, cols] = gt
        xs, gs = [], []
        for h in range(G):
            rows = slice(h * size, (h + 1) * size)
            xs.append((xt[rows].astype(F32) * scaled[h : h + 1]).astype(BF16))
            gs.append((gt[rows].astype(F32) * grown[h : h + 1]).astype(BF16))
        fresh.append(fdot(jnp.concatenate(xs, 0), bmap[cols, :]))
        read.append(fdot(jnp.concatenate(gs, 0), cmap[cols, :]))
        ends.append(end)
    total = ends[0]
    for c in range(1, blocks):
        fresh_out[c - 1] = fresh[c - 1]
        read_out[c - 1] = read[c]
        total = total + ends[c]
    esum_out[...] = jnp.broadcast_to(total, esum_out.shape)
    for h in range(G):
        rows = slice(h * size, (h + 1) * size)
        state = fresh[0][rows]
        cot = read[-1][rows]
        for c in range(1, blocks):
            state = jnp.exp(ends[c][h : h + 1]) * state + fresh[c][rows]
            back = blocks - 1 - c
            cot = jnp.exp(ends[back][h : h + 1]) * cot + read[back][rows]
        for k, payload in enumerate(payloads):
            payload[rows, :] = jnp.where(flags[k] == 0, state, cot)


def intra_kernel(size, steps, logs, g, xt, gt, bmap, cmap, gf_out, rowsum, colsum, skip,
                 gin, gout, scores, total):
    i = pl.program_id(0)
    blocks = steps.shape[1] // Q
    half = Q // 2

    @pl.when(i == 0)
    def _():
        row = lax.broadcasted_iota(jnp.int32, (Q, Q), 0)
        col = lax.broadcasted_iota(jnp.int32, (Q, Q), 1)
        for c in range(blocks):
            cols = slice(c * Q, (c + 1) * Q)
            s = lax.dot_general(cmap[cols, :], bmap[cols, :], NT, preferred_element_type=F32)
            scores[c] = jnp.where(row >= col, s, 0.0)
        total[...] = jnp.zeros_like(total)

    lane = lax.broadcasted_iota(jnp.int32, (Q, 2 * size), 1)
    for c in range(blocks):
        cols = slice(c * Q, (c + 1) * Q)
        base = c * Q
        lrow = logs[:, cols] * LOG2E
        lcol = lrow.T
        srow = steps[:, cols]
        acc0 = total[c, :half, :half]
        acc1 = total[c, half:, :]
        sums, col_parts, skips = [], [], []
        for h in range(G):
            pair = slice(h // 2 * 2 * size, (h // 2 + 1) * 2 * size)
            rows = slice(h * size, (h + 1) * size)
            mine = lane < size if h % 2 == 0 else lane >= size
            gm = jnp.where(mine, g[cols, pair], jnp.zeros((), BF16))
            row_parts = []
            mixes = []
            column = None
            for slab in range(2):
                ts = slice(slab * half, (slab + 1) * half)
                width = (slab + 1) * half
                ss = slice(0, width)
                inner = fdot(gm[ts], xt[pair, base : base + width])
                spread = jnp.minimum(lcol[ts, h : h + 1] - lrow[h : h + 1, ss], 0.0)
                kern = jnp.exp2(spread) * scores[c, ts, ss]
                step = srow[h : h + 1, ss]
                mixes.append((kern * step).astype(BF16))
                weighted = kern * inner
                pulled = weighted * step
                if slab == 0:
                    acc0 = acc0 + pulled
                else:
                    acc1 = acc1 + pulled
                row_parts.append(jnp.sum(pulled, axis=1, keepdims=True))
                part = jnp.sum(weighted, axis=0, keepdims=True)
                if slab == 0:
                    column = jnp.concatenate([part, jnp.zeros_like(part)], 1)
                else:
                    column = column + part
            col_parts.append(column)
            sums.append(jnp.concatenate(row_parts, 0))
            low = fdot(gt[rows, base : base + half], mixes[0])
            full = fdot(gt[rows, base + half : base + Q], mixes[1])
            gf_out[rows, base : base + half] = low + full[:, :half]
            gf_out[rows, base + half : base + Q] = full[:, half:]
            both = gt[rows, cols].astype(F32) * xt[rows, cols].astype(F32)
            skips.append(jnp.sum(both, axis=0, keepdims=True))
        total[c, :half, :half] = acc0
        total[c, half:, :] = acc1
        colsum[:, cols] = jnp.concatenate(col_parts, 0)
        rowsum[:, cols] = jnp.concatenate(sums, 1).T
        skip[:, cols] = jnp.concatenate(skips, 0)

    @pl.when(i == pl.num_programs(0) - 1)
    def _():
        for c in range(blocks):
            cols = slice(c * Q, (c + 1) * Q)
            grads = total[c].astype(BF16)
            gin[cols, :] = lax.dot_general(grads, cmap[cols, :], TN, preferred_element_type=F32)
            gout[cols, :] = fdot(grads, bmap[cols, :])


def finish_kernel(size, count, weights, gains, steps, rates, logs, rowsum, colsum, skip, xt, gt,
                  gf_in, bmap, cmap, gin, gout, first, last, fresh, read, *rest):
    received = rest[:count]
    gf, gsteps, gin_all, gout_all, rate_part, skip_part, tin, tout = rest[count:]
    i = pl.program_id(0)
    blocks = steps.shape[1] // Q
    suffix = tri("suffix")

    @pl.when(i == 0)
    def _():
        tin[...] = jnp.zeros_like(tin)
        tout[...] = jnp.zeros_like(tout)

    ends = [logs[:, (c + 1) * Q - 1 : (c + 1) * Q] for c in range(blocks)]
    entering = [[None] * G for _ in range(blocks)]
    leaving = [[None] * G for _ in range(blocks)]
    for h in range(G):
        head = i * G + h
        rows = slice(h * size, (h + 1) * size)
        state = weights[0, 0, head] * first[rows].astype(F32)
        cot = weights[1, 0, head] * last[rows].astype(F32)
        for d in range(count):
            value = received[d][rows]
            state = state + weights[0, d + 1, head] * value
            cot = cot + weights[1, d + 1, head] * value
        entering[0][h] = state
        leaving[-1][h] = cot
        for c in range(1, blocks):
            entering[c][h] = jnp.exp(ends[c - 1][h : h + 1]) * entering[c - 1][h] + fresh[c - 1, rows]
            b = blocks - 1 - c
            leaving[b][h] = jnp.exp(ends[b + 1][h : h + 1]) * leaving[b + 1][h] + read[b, rows]
    rate_total = jnp.zeros((G, 1), F32)
    lane = lax.broadcasted_iota(jnp.int32, (1, Q), 1)
    for c in range(blocks):
        cols = slice(c * Q, (c + 1) * Q)
        log = logs[:, cols]
        step = steps[:, cols]
        decay = jnp.exp(ends[c] - log)
        scaled = decay * step
        grown = jnp.exp(log)
        eb = jnp.concatenate([e.astype(BF16) for e in entering[c]], 0)
        lb = jnp.concatenate([e.astype(BF16) for e in leaving[c]], 0)
        out_t = lax.dot_general(eb, cmap[cols, :], NT, preferred_element_type=F32)
        in_t = lax.dot_general(lb, bmap[cols, :], NT, preferred_element_type=F32)
        xs, gs, rdots, idots, prods = [], [], [], [], []
        for h in range(G):
            rows = slice(h * size, (h + 1) * size)
            xh = xt[rows, cols].astype(F32)
            gh = gt[rows, cols].astype(F32)
            sc = scaled[h : h + 1]
            xs.append((xh * sc).astype(BF16))
            gs.append((gh * grown[h : h + 1]).astype(BF16))
            rdots.append(jnp.sum(gh * out_t[rows], axis=0, keepdims=True))
            idots.append(jnp.sum(xh * in_t[rows], axis=0, keepdims=True))
            prods.append(jnp.sum(leaving[c][h] * entering[c][h], axis=0, keepdims=True))
            grad = gf_in[rows, cols] + sc * in_t[rows] + gains[i * G + h] * gh
            gf[cols, rows] = grad.T.astype(BF16)
        tin[:, cols] += lax.dot_general(lb, jnp.concatenate(xs, 0), TN, preferred_element_type=F32)
        tout[:, cols] += lax.dot_general(eb, jnp.concatenate(gs, 0), TN, preferred_element_type=F32)
        rdot = jnp.concatenate(rdots, 0)
        idot = jnp.concatenate(idots, 0)
        prod = jnp.sum(jnp.concatenate(prods, 0), axis=1, keepdims=True)
        terms = scaled * idot
        extra = jnp.sum(terms, axis=1, keepdims=True) + jnp.exp(ends[c]) * prod
        weighted = colsum[:, cols]
        logs_grad = rowsum[:, cols] - step * weighted + grown * rdot - terms
        logs_grad = logs_grad + jnp.where(lane == Q - 1, extra, 0.0)
        through = exact_dot(logs_grad, suffix)
        gsteps[:, cols] = rates[...] * through + weighted + decay * idot
        rate_total = rate_total + jnp.sum(step * through, axis=1, keepdims=True)
    rate_part[...] = rates[...] * rate_total
    skip_part[...] = jnp.sum(skip[...], axis=1, keepdims=True)

    @pl.when(i == pl.num_programs(0) - 1)
    def _():
        gin_all[...] = gin[...] + tin[...].T
        gout_all[...] = gout[...] + tout[...].T


def local(features, step_sizes, rate_logs, input_map, output_map, skip_gain, state_first,
          upstream, state_last):
    heads = rate_logs.shape[0]
    length = features.shape[1]
    size = features.shape[2] // heads
    dim = input_map.shape[2]
    blocks = length // Q
    x, g, steps = features[0], upstream[0], step_sizes[0]
    bmap, cmap = input_map[0], output_map[0]
    rates = -jnp.exp(rate_logs)[:, None]
    n = lax.axis_size("ctx")
    me = lax.axis_index("ctx")
    levels = n.bit_length() - 1
    flags = (me >> jnp.arange(max(levels, 1))) & 1
    wide = G * size
    grid = (heads // G,)
    params = pltpu.CompilerParams(vmem_limit_bytes=56 * 1024 * 1024)
    smem = pl.BlockSpec(memory_space=pltpu.SMEM)
    head_rows = pl.BlockSpec((G, length), lambda i: (i, 0))
    rate_rows = pl.BlockSpec((G, 1), lambda i: (i, 0))
    natural = pl.BlockSpec((length, wide), lambda i: (0, i))
    turned = pl.BlockSpec((wide, length), lambda i: (i, 0))
    whole = pl.BlockSpec((length, dim), lambda i: (0, 0))
    state = pl.BlockSpec((wide, dim), lambda i: (i, 0))
    inner = pl.BlockSpec((blocks - 1, wide, dim), lambda i: (0, i, 0))
    state_shape = jax.ShapeDtypeStruct((heads * size, dim), F32)
    inner_shape = jax.ShapeDtypeStruct((blocks - 1, heads * size, dim), F32)
    row_shape = jax.ShapeDtypeStruct((heads, length), F32)
    map_shape = jax.ShapeDtypeStruct((length, dim), F32)
    one_shape = jax.ShapeDtypeStruct((heads, 1), F32)
    turned_shape = jax.ShapeDtypeStruct((heads * size, length), BF16)
    fresh, read, logs, esum, xt, gt, *payloads = pl.pallas_call(
        partial(states_kernel, size),
        grid=grid,
        in_specs=[smem, head_rows, rate_rows, natural, natural, whole, whole],
        out_specs=[inner, inner, head_rows, rate_rows, turned, turned] + [state] * levels,
        out_shape=[inner_shape, inner_shape, row_shape, one_shape, turned_shape, turned_shape]
        + [state_shape] * levels,
        compiler_params=params,
        name="states",
        cost_estimate=pl.CostEstimate(flops=10**9, bytes_accessed=14 * 10**6, transcendentals=0),
    )(flags, steps, rates, x, g, bmap, cmap)

    received, sums = [], []
    for d in range(1, n):
        pairs = [(i, i ^ d) for i in range(n)]
        received.append(lax.ppermute(payloads[d.bit_length() - 1], "ctx", pairs))
        sums.append(lax.ppermute(esum, "ctx", pairs))

    gf_in, rowsum, colsum, skip, gin, gout = pl.pallas_call(
        partial(intra_kernel, size),
        grid=grid,
        in_specs=[head_rows, head_rows, natural, turned, turned, whole, whole],
        out_specs=[turned, head_rows, head_rows, head_rows, whole, whole],
        out_shape=[jax.ShapeDtypeStruct((heads * size, length), F32), row_shape, row_shape,
                   row_shape, map_shape, map_shape],
        scratch_shapes=[pltpu.VMEM((blocks, Q, Q), F32)] * 2,
        compiler_params=params,
        name="intra",
        cost_estimate=pl.CostEstimate(flops=2 * 10**10, bytes_accessed=16 * 10**6,
                                      transcendentals=0),
    )(steps, logs, g, xt, gt, bmap, cmap)

    others = jnp.arange(n)
    by_distance = jnp.stack([esum[:, 0]] + [s[:, 0] for s in sums])
    by_place = by_distance[others ^ me]
    source = (me ^ others)[:, None]
    between = others[None, :]
    ahead = (source < between) & (between < me)
    behind = (me < between) & (between < source)
    fore = jnp.where(source < me, jnp.exp(jnp.where(ahead[:, :, None], by_place[None], 0.0).sum(1)), 0.0)
    aft = jnp.where(source > me, jnp.exp(jnp.where(behind[:, :, None], by_place[None], 0.0).sum(1)), 0.0)
    enter = jnp.exp(jnp.where((others < me)[:, None], by_place, 0.0).sum(0))
    leave = jnp.exp(jnp.where((others > me)[:, None], by_place, 0.0).sum(0))
    weights = jnp.stack([fore.at[0].set(enter), aft.at[0].set(leave)])

    gf, gsteps, gin, gout, rate_part, skip_part = pl.pallas_call(
        partial(finish_kernel, size, n - 1),
        grid=grid,
        in_specs=[smem, smem, head_rows, rate_rows, head_rows, head_rows, head_rows, head_rows,
                  turned, turned, turned, whole, whole, whole, whole, state, state, inner, inner]
        + [state] * (n - 1),
        out_specs=[natural, head_rows, whole, whole, rate_rows, rate_rows],
        out_shape=[jax.ShapeDtypeStruct((length, heads * size), BF16), row_shape, map_shape,
                   map_shape, one_shape, one_shape],
        scratch_shapes=[pltpu.VMEM((dim, length), F32)] * 2,
        compiler_params=params,
        name="finish",
        cost_estimate=pl.CostEstimate(flops=2 * 10**9, bytes_accessed=30 * 10**6,
                                      transcendentals=0),
    )(weights, skip_gain, steps, rates, logs, rowsum, colsum, skip, xt, gt, gf_in, bmap, cmap,
      gin, gout, state_first[0].reshape(heads * size, dim), state_last[0].reshape(heads * size, dim),
      fresh, read, *received)
    sums = lax.psum(jnp.concatenate([rate_part[:, 0], skip_part[:, 0]]), ("ctx", "seq"))
    return (gf[None], gsteps[None], gin[None], gout[None], sums[:heads], sums[heads:])


def solution(mesh):
    tokens = P("seq", "ctx", None)
    state = P("seq", None, None, None)
    head_tokens = P("seq", None, "ctx")
    return jax.shard_map(
        local,
        mesh=mesh,
        in_specs=(tokens, head_tokens, P(), tokens, tokens, P(), state, tokens, state),
        out_specs=(tokens, head_tokens, tokens, tokens, P(), P()),
        check_vma=False,
    )
```

time: 370 us -> 137 us (0.37)
  local copies, waits for them, and re-layouts: 130 us -> 3.36 us
  matrix products: 62.1 us -> 0 us
  waiting for transfers between devices: 87.7 us -> 27.3 us
  Pallas kernels: 0 us -> 52.8 us
  other arithmetic: 53.7 us -> 4.44 us
  blocking collectives: 23.2 us -> 39.6 us
    dot_general x22 -> x0, matrix products: 62.1 us -> none  [the longest x2 18.7 us: block_local(): jnp.einsum('thp,shp->hts', upstream, inputs, preferred_element_type=jnp.f...]
    ppermute x6, waiting for transfers between devices: 87.7 us -> 27.3 us  [the longest x3 27.3 us: local(): received.append(lax.ppermute(payloads[d.bit_length() - 1], 'ctx', pairs))]
    pallas_call x0 -> x3, Pallas kernels: none -> 52.8 us  [the longest x1 30.1 us: local(): pl.pallas_call(partial(intra_kernel, size), grid=grid, in_specs=[head_row...]
    dot_general x2 -> x0, local copies, waits for them, and re-layouts: 41.4 us -> none  [block_local(): jnp.einsum('thp,shp->hts', upstream, inputs, preferred_element_type=jnp.f...]
    add x12 -> x0, other arithmetic: 29.1 us -> none  [the longest x8 22.5 us: enter_block(): return (jnp.exp(end_log)[:, None, None] * running + fresh_block, running)]
    another operation x28 -> x0, local copies, waits for them, and re-layouts: 25 us -> none
    while x86 -> x0, local copies, waits for them, and re-layouts: 19.4 us -> none  [the longest x2 11.7 us: local(): lax.map(partial(block_local, decay_rates=decay_rates), stacked)]
    psum x2 -> x1, blocking collectives: 23.2 us -> 39.6 us  [local(): lax.psum(jnp.concatenate([rate_part[:, 0], skip_part[:, 0]]), ('ctx', 'se...]
  transfers between devices with their start and end apart: 6 -> 6, of which waited for: 3 -> 1; matrix products, arithmetic and copies ran while one was open for 6% -> 2% of each run, Pallas kernels for 0% -> 22%
where the time goes in v1:
time: 137 us; the launch traced here: 136 us
  Pallas kernels  52.8 us (39%)
  blocking collectives  39.6 us (29%)
  waiting for transfers between devices  27.3 us (20%)
  starting transfers between devices  8.16 us (6%)
  other arithmetic  4.44 us (3%)
  local copies, waits for them, and re-layouts  3.36 us (2%)
    psum x1, blocking collectives, local(): lax.psum(jnp.concatenate([rate_part[:, 0], skip_part[:, 0]]), ('ctx', 'se...  39.6 us
    pallas_call x1, Pallas kernels, local(): pl.pallas_call(partial(intra_kernel, size), grid=grid, in_specs=[head_row...  30.1 us
    ppermute x3, waiting for transfers between devices, local(): received.append(lax.ppermute(payloads[d.bit_length() - 1], 'ctx', pairs))  27.3 us
    pallas_call x1, Pallas kernels, local(): pl.pallas_call(partial(finish_kernel, size, n - 1), grid=grid, in_specs=[...  13.1 us
    pallas_call x1, Pallas kernels, local(): pl.pallas_call(partial(states_kernel, size), grid=grid, in_specs=[smem, h...  9.56 us
    ppermute x3, starting transfers between devices, local(): sums.append(lax.ppermute(esum, 'ctx', pairs))  4.6 us
    ppermute x3, starting transfers between devices, local(): received.append(lax.ppermute(payloads[d.bit_length() - 1], 'ctx', pairs))  3.56 us
  transfers between devices with their start and end apart: 6, of which 1 were waited for; matrix products, arithmetic and copies ran while one was open for 2% of the time, Pallas kernels for 22%

profile of v1, /device:TPU:0, one launch (start us, length us, event | category | flops | bytes accessed | tf_op | source)
XLA Modules:
  0.0 136.4 jit_solution(13855789490121958104)
XLA Ops:
  0.6 0.7 negate_bitcast_fusion
  1.3 0.5 shift-right-arithmetic_and_fusion.flags
  1.8 0.7 copy.19.rates
  2.5 9.6 %states.1 = (f32[1,2560,128]{2,1,0:T(8,128)}, f32[1,2560,128]{2,1,0:T(8,128)}, f32[40,512]{1,0:T(8,128)}, f32[40,1]{1,0:T(8,128)}, bf16[2560,512]{1,0:T(8,128)(2...) custom-call(s32[2]{0:T(128)} %shift-right-arithmetic_and_fusion.flags, ...), custom_call_target="tpu_custom_call" | custom-call | flops 1000000000 | bytes 14000000 | tf_op jit(solution)/shard_map/states/pallas_call | solution.py:265
  12.1 4.0 %collective-permute-start.2 = (f32[40,1]{1,0:T(8,128)}, f32[40,1]{1,0:T(8,128)S(1)}, u32[]{:S(2)}, u32[]{:S(2)}) collective-permute-start(f32[40,1]{1,0:T(8,128)} %get-tuple-element.50), channel_id=1, source_target_pairs={{0,3},{1,2},{2,1},{3,0},{4,7},{5,6},{6,5},{7,4},{8,11},{9,10},{10,... | collective-permute-start | bytes 488 | tf_op jit(solution)/shard_map/ppermute | solution.py:281
  16.0 0.5 collective-permute-start.1
  16.5 0.1 collective-permute-start
  16.7 2.8 %collective-permute-start.5 = (f32[2560,128]{1,0:T(8,128)}, f32[2560,128]{1,0:T(8,128)S(1)}, u32[]{:S(2)}, u32[]{:S(2)}) collective-permute-start(f32[2560,128]{1,0:T(8,128)} %get-tuple-element.63), channel_id=1, source_target_pairs={{0,3},{1,2},{2,1},{3,0},{4,7},{5,6},{6,5},{7,4},{8,11},{9,10},{10,... | collective-permute-start | bytes 3932168 | tf_op jit(solution)/shard_map/ppermute | solution.py:280
  19.5 0.5 collective-permute-start.4
  20.1 0.1 fusion.1
  20.2 0.0 copy-start.2
  20.2 30.1 %intra.1 = (f32[2560,512]{1,0:T(8,128)}, f32[40,512]{1,0:T(8,128)}, f32[40,512]{1,0:T(8,128)}, f32[40,512]{1,0:T(8,128)}, f32[512,128]{1,0:T(8,128)}, /*index=5*/f32[512,128]{1,0:T(8,128)}) custom-call(f32[40,512]{1,0:T(8,128)} %bitcast.39, f32[40,512]{1,0:T(8,128)} %get-tuple-element.51.logs, bf16[512,2560]{1,0:T(8,128)(2,1)} %bitcast.29, ...), custom_call_target="tpu_custom_call" | custom-call | flops 20000000000 | bytes 16000000 | tf_op jit(solution)/shard_map/intra/pallas_call | solution.py:283
  50.2 0.0 copy-done.2
  50.2 0.1 reduce.4
  50.4 0.0 collective-permute-done.2
  50.4 0.2 collective-permute-start.3
  50.6 0.1 reduce.7
  50.7 0.0 collective-permute-done.1
  50.7 0.1 reduce.6
  50.8 0.0 collective-permute-done
  50.8 0.1 reduce.5
  50.9 0.6 gather_fusion
  51.5 0.1 select_reduce_fusion.3
  51.6 0.1 select_reduce_fusion.1
  51.7 0.1 bitcast_select_fusion.1
  51.8 0.1 bitcast_select_fusion
  51.9 0.6 pad_maximum_fusion.weights
  52.5 27.3 %collective-permute-done.3.rest_0_ = f32[2560,128]{1,0:T(8,128)} collective-permute-done((f32[2560,128]{1,0:T(8,128)}, f32[2560,128]{1,0:T(8,128)}, u32[]{:S(2)}, u32[]{:S(2)}) %collective-permute-start.3) | collective-permute-done | bytes 1310752 | tf_op jit(solution)/shard_map/ppermute | solution.py:280
  79.9 0.0 collective-permute-done.5.rest_2_
  79.9 0.0 copy-start
  79.9 0.0 collective-permute-done.4.rest_1_
  79.9 0.0 copy-start.1
  79.9 1.0 copy-done
  80.9 0.4 copy-done.1
  81.3 13.1 %finish.1 = (bf16[512,2560]{1,0:T(8,128)(2,1)}, f32[40,512]{1,0:T(8,128)}, f32[512,128]{1,0:T(8,128)}, f32[512,128]{1,0:T(8,128)}, f32[40,1]{1,0:T(8,128)}, /*index=5*/f32[40,1]{1,0:T(8,128)}) custom-call(f32[2,4,40]{2,1,0:T(4,128)} %pad_maximum_fusion.weights, f32[40]{0:T(128)} %gains.1, f32[40,512]{1,0:T(8,128)} %bitcast.40, f32[40,1]{1,0:T(8,128)} %copy.19.rates, ...), custom_call_target="tpu_custom_call" | custom-call | flops 2000000000 | bytes 30000000 | tf_op jit(solution)/shard_map/finish/pallas_call | solution.py:310
  94.5 0.8 reduce.8
  95.3 0.8 reduce.9
  96.2 0.1 pad_maximum_fusion.2
  96.2 39.6 %psum.7 = f32[80]{0:T(128)S(1)} all-reduce(f32[80]{0:T(128)S(1)} %pad_maximum_fusion.2), channel_id=1, replica_groups=mesh['seq'=8,'ctx'=4] {'ctx','seq'}, use_global_device_ids=true, to_apply=%region_4.5 | all-reduce | flops 80 | bytes 640 | tf_op jit(solution)/shard_map/psum | solution.py:327
  135.8 0.6 fusion.3
  (11 shorter events, 0.1 us)
Async XLA Ops:
  12.1 38.3 %collective-permute-start.2 = (f32[40,1]{1,0:T(8,128)}, f32[40,1]{1,0:T(8,128)S(1)}, u32[]{:S(2)}, u32[]{:S(2)}) collective-permute-start(f32[40,1]{1,0:T(8,128)} %get-tuple-element.50), channel_id=1, source_target_pairs={{0,3},{1,2},{2,1},{3,0},{4,7},{5,6},{6,5},{7,4},{8,11},{9,10},{10,... | collective-permute-start | bytes 488 | tf_op jit(solution)/shard_map/ppermute | solution.py:281
  16.0 34.6 %collective-permute-start.1 = (f32[40,1]{1,0:T(8,128)}, f32[40,1]{1,0:T(8,128)S(1)}, u32[]{:S(2)}, u32[]{:S(2)}) collective-permute-start(f32[40,1]{1,0:T(8,128)} %get-tuple-element.50), channel_id=1, source_target_pairs={{0,2},{1,3},{2,0},{3,1},{4,6},{5,7},{6,4},{7,5},{8,10},{9,11},{10,... | collective-permute-start | bytes 488 | tf_op jit(solution)/shard_map/ppermute | solution.py:281
  16.5 34.3 %collective-permute-start = (f32[40,1]{1,0:T(8,128)}, f32[40,1]{1,0:T(8,128)S(1)}, u32[]{:S(2)}, u32[]{:S(2)}) collective-permute-start(f32[40,1]{1,0:T(8,128)} %get-tuple-element.50), channel_id=1, source_target_pairs={{0,1},{1,0},{2,3},{3,2},{4,5},{5,4},{6,7},{7,6},{8,9},{9,8},{10,11... | collective-permute-start | bytes 488 | tf_op jit(solution)/shard_map/ppermute | solution.py:281
  16.7 63.2 %collective-permute-start.5 = (f32[2560,128]{1,0:T(8,128)}, f32[2560,128]{1,0:T(8,128)S(1)}, u32[]{:S(2)}, u32[]{:S(2)}) collective-permute-start(f32[2560,128]{1,0:T(8,128)} %get-tuple-element.63), channel_id=1, source_target_pairs={{0,3},{1,2},{2,1},{3,0},{4,7},{5,6},{6,5},{7,4},{8,11},{9,10},{10,... | collective-permute-start | bytes 3932168 | tf_op jit(solution)/shard_map/ppermute | solution.py:280
  19.5 60.3 %collective-permute-start.4 = (f32[2560,128]{1,0:T(8,128)}, f32[2560,128]{1,0:T(8,128)S(1)}, u32[]{:S(2)}, u32[]{:S(2)}) collective-permute-start(f32[2560,128]{1,0:T(8,128)} %get-tuple-element.63), channel_id=1, source_target_pairs={{0,2},{1,3},{2,0},{3,1},{4,6},{5,7},{6,4},{7,5},{8,10},{9,11},{10,... | collective-permute-start | bytes 3932168 | tf_op jit(solution)/shard_map/ppermute | solution.py:280
  20.2 30.1 %copy-start.2 = (f32[40,1]{1,0:T(8,128)S(1)}, f32[40,1]{1,0:T(8,128)}, u32[]{:S(2)}) copy-start(f32[40,1]{1,0:T(8,128)} %get-tuple-element.50) | copy-start | bytes 484
  50.4 29.5 %collective-permute-start.3 = (f32[2560,128]{1,0:T(8,128)}, f32[2560,128]{1,0:T(8,128)}, u32[]{:S(2)}, u32[]{:S(2)}) collective-permute-start(f32[2560,128]{1,0:T(8,128)} %get-tuple-element.62), channel_id=1, source_target_pairs={{0,1},{1,0},{2,3},{3,2},{4,5},{5,4},{6,7},{7,6},{8,9},{9,8},{10,11... | collective-permute-start | bytes 3932168 | tf_op jit(solution)/shard_map/ppermute | solution.py:280
  79.9 1.1 copy-start
  79.9 1.4 %copy-start.1 = (f32[2560,128]{1,0:T(8,128)}, f32[2560,128]{1,0:T(8,128)S(1)}, u32[]{:S(2)}) copy-start(f32[2560,128]{1,0:T(8,128)S(1)} %collective-permute-done.4.rest_1_) | copy-start | bytes 3932164

commit v2 on v1

--- a/solution.py
+++ b/solution.py
@@ -30,9 +30,9 @@
     return (row <= col if kind == "prefix" else row >= col).astype(F32)
 
 
-def states_kernel(size, flags, steps, rates, x, g, bmap, cmap, *outs):
-    fresh_out, read_out, ls_out, esum_out, xt_out, gt_out = outs[:6]
-    payloads = outs[6:]
+def states_kernel(size, held, flags, steps, rates, x, g, bmap, cmap, *rest):
+    ls_out, xt_out, gt_out, fresh_out, read_out = rest[held : held + 5]
+    payloads = rest[held + 5 :]
     blocks = steps.shape[1] // Q
     prefix = tri("prefix")
     fresh, read, ends = [], [], []
@@ -56,12 +56,9 @@
         fresh.append(fdot(jnp.concatenate(xs, 0), bmap[cols, :]))
         read.append(fdot(jnp.concatenate(gs, 0), cmap[cols, :]))
         ends.append(end)
-    total = ends[0]
     for c in range(1, blocks):
         fresh_out[c - 1] = fresh[c - 1]
         read_out[c - 1] = read[c]
-        total = total + ends[c]
-    esum_out[...] = jnp.broadcast_to(total, esum_out.shape)
     for h in range(G):
         rows = slice(h * size, (h + 1) * size)
         state = fresh[0][rows]
@@ -152,10 +149,10 @@
             gout[cols, :] = fdot(grads, bmap[cols, :])
 
 
-def finish_kernel(size, count, weights, gains, steps, rates, logs, rowsum, colsum, skip, xt, gt,
+def finish_kernel(size, count, base, held, weights, gains, steps, rates, logs, rowsum, colsum, skip, xt, gt,
                   gf_in, bmap, cmap, gin, gout, first, last, fresh, read, *rest):
     received = rest[:count]
-    gf, gsteps, gin_all, gout_all, rate_part, skip_part, tin, tout = rest[count:]
+    gf, gsteps, gin_all, gout_all, rate_part, skip_part, tin, tout = rest[count + held :]
     i = pl.program_id(0)
     blocks = steps.shape[1] // Q
     suffix = tri("suffix")
@@ -169,7 +166,7 @@
     entering = [[None] * G for _ in range(blocks)]
     leaving = [[None] * G for _ in range(blocks)]
     for h in range(G):
-        head = i * G + h
+        head = (base + i) * G + h
         rows = slice(h * size, (h + 1) * size)
         state = weights[0, 0, head] * first[rows].astype(F32)
         cot = weights[1, 0, head] * last[rows].astype(F32)
@@ -207,7 +204,7 @@
             rdots.append(jnp.sum(gh * out_t[rows], axis=0, keepdims=True))
             idots.append(jnp.sum(xh * in_t[rows], axis=0, keepdims=True))
             prods.append(jnp.sum(leaving[c][h] * entering[c][h], axis=0, keepdims=True))
-            grad = gf_in[rows, cols] + sc * in_t[rows] + gains[i * G + h] * gh
+            grad = gf_in[rows, cols] + sc * in_t[rows] + gains[(base + i) * G + h] * gh
             gf[cols, rows] = grad.T.astype(BF16)
         tin[:, cols] += lax.dot_general(lb, jnp.concatenate(xs, 0), TN, preferred_element_type=F32)
         tout[:, cols] += lax.dot_general(eb, jnp.concatenate(gs, 0), TN, preferred_element_type=F32)
@@ -231,6 +228,54 @@
         gout_all[...] = gout[...] + tout[...].T
 
 
+def sums_kernel(n, m, parts, *refs):
+    rates, skips = refs[:parts], refs[parts : 2 * parts]
+    out, mine, first, second, send1, recv1, send2, recv2 = refs[2 * parts :]
+    here, there = lax.axis_index("ctx"), lax.axis_index("seq")
+    barrier = pltpu.get_barrier_semaphore()
+    for d in range(1, n):
+        pl.semaphore_signal(barrier, inc=1, device_id={"ctx": lax.rem(here + d, n)},
+                            device_id_type=pl.DeviceIdType.MESH)
+    for d in range(1, m):
+        pl.semaphore_signal(barrier, inc=1, device_id={"seq": lax.rem(there + d, m)},
+                            device_id_type=pl.DeviceIdType.MESH)
+    heads = out.shape[1]
+    row = lax.broadcasted_iota(jnp.int32, (heads, heads), 0)
+    col = lax.broadcasted_iota(jnp.int32, (heads, heads), 1)
+    mine[...] = jnp.zeros_like(mine)
+    for k, group in enumerate((rates, skips)):
+        column = jnp.concatenate([r[...] for r in group], 0)
+        line = jnp.sum(jnp.where(row == col, column, 0.0), axis=0, keepdims=True)
+        mine[k : k + 1, :heads] = line
+    pl.semaphore_wait(barrier, n + m - 2)
+
+    def exchange(axis, place, count, slots, send, recv):
+        copies = []
+        slots[place] = mine[...]
+        for d in range(1, count):
+            copy = pltpu.make_async_remote_copy(
+                src_ref=mine, dst_ref=slots.at[place], send_sem=send.at[d],
+                recv_sem=recv.at[place], device_id={axis: lax.rem(place + d, count)},
+                device_id_type=pl.DeviceIdType.MESH)
+            copy.start()
+            copies.append(copy)
+        for d in range(1, count):
+            source = lax.rem(place + count - d, count)
+            pltpu.make_async_remote_copy(
+                src_ref=mine, dst_ref=slots.at[source], send_sem=send.at[d],
+                recv_sem=recv.at[source], device_id={axis: source},
+                device_id_type=pl.DeviceIdType.MESH).wait_recv()
+        for copy in copies:
+            copy.wait_send()
+        total = slots[0]
+        for k in range(1, count):
+            total = total + slots[k]
+        return total
+
+    mine[...] = exchange("ctx", here, n, first, send1, recv1)
+    out[...] = exchange("seq", there, m, second, send2, recv2)[:2, :heads]
+
+
 def local(features, step_sizes, rate_logs, input_map, output_map, skip_gain, state_first,
           upstream, state_last):
     heads = rate_logs.shape[0]
@@ -240,51 +285,70 @@
     blocks = length // Q
     x, g, steps = features[0], upstream[0], step_sizes[0]
     bmap, cmap = input_map[0], output_map[0]
+    first = state_first[0].reshape(heads * size, dim)
+    last = state_last[0].reshape(heads * size, dim)
     rates = -jnp.exp(rate_logs)[:, None]
-    n = lax.axis_size("ctx")
+    n, m = lax.axis_size("ctx"), lax.axis_size("seq")
     me = lax.axis_index("ctx")
     levels = n.bit_length() - 1
     flags = (me >> jnp.arange(max(levels, 1))) & 1
     wide = G * size
-    grid = (heads // G,)
+    groups = heads // G
+    chunks = [(0, groups)]
     params = pltpu.CompilerParams(vmem_limit_bytes=56 * 1024 * 1024)
     smem = pl.BlockSpec(memory_space=pltpu.SMEM)
-    head_rows = pl.BlockSpec((G, length), lambda i: (i, 0))
-    rate_rows = pl.BlockSpec((G, 1), lambda i: (i, 0))
-    natural = pl.BlockSpec((length, wide), lambda i: (0, i))
-    turned = pl.BlockSpec((wide, length), lambda i: (i, 0))
+    anywhere = pl.BlockSpec(memory_space=pl.ANY)
     whole = pl.BlockSpec((length, dim), lambda i: (0, 0))
-    state = pl.BlockSpec((wide, dim), lambda i: (i, 0))
-    inner = pl.BlockSpec((blocks - 1, wide, dim), lambda i: (0, i, 0))
-    state_shape = jax.ShapeDtypeStruct((heads * size, dim), F32)
-    inner_shape = jax.ShapeDtypeStruct((blocks - 1, heads * size, dim), F32)
+
+    def specs(base):
+        return (
+            pl.BlockSpec((G, length), lambda i: (base + i, 0)),
+            pl.BlockSpec((G, 1), lambda i: (base + i, 0)),
+            pl.BlockSpec((length, wide), lambda i: (0, base + i)),
+            pl.BlockSpec((wide, length), lambda i: (base + i, 0)),
+            pl.BlockSpec((wide, dim), lambda i: (base + i, 0)),
+            pl.BlockSpec((blocks - 1, wide, dim), lambda i: (0, base + i, 0)),
+        )
+
+    head_rows0, rate_rows0, natural0, turned0, state0, inner0 = specs(0)
     row_shape = jax.ShapeDtypeStruct((heads, length), F32)
     map_shape = jax.ShapeDtypeStruct((length, dim), F32)
-    one_shape = jax.ShapeDtypeStruct((heads, 1), F32)
     turned_shape = jax.ShapeDtypeStruct((heads * size, length), BF16)
-    fresh, read, logs, esum, xt, gt, *payloads = pl.pallas_call(
-        partial(states_kernel, size),
-        grid=grid,
-        in_specs=[smem, head_rows, rate_rows, natural, natural, whole, whole],
-        out_specs=[inner, inner, head_rows, rate_rows, turned, turned] + [state] * levels,
-        out_shape=[inner_shape, inner_shape, row_shape, one_shape, turned_shape, turned_shape]
-        + [state_shape] * levels,
-        compiler_params=params,
-        name="states",
-        cost_estimate=pl.CostEstimate(flops=10**9, bytes_accessed=14 * 10**6, transcendentals=0),
-    )(flags, steps, rates, x, g, bmap, cmap)
-
-    received, sums = [], []
-    for d in range(1, n):
-        pairs = [(i, i ^ d) for i in range(n)]
-        received.append(lax.ppermute(payloads[d.bit_length() - 1], "ctx", pairs))
-        sums.append(lax.ppermute(esum, "ctx", pairs))
+
+    esum = jnp.sum(steps, axis=1, keepdims=True) * rates
+    pairs = [[(i, i ^ d) for i in range(n)] for d in range(n)]
+    sums = [lax.ppermute(esum, "ctx", pairs[d]) for d in range(1, n)]
+
+    shared, states = (), []
+    for base, width in chunks:
+        head_rows, rate_rows, natural, turned, state, inner = specs(base)
+        held = len(shared)
+        inner_shape = jax.ShapeDtypeStruct((blocks - 1, width * wide, dim), F32)
+        *shared, fresh, read = results = pl.pallas_call(
+            partial(states_kernel, size, held),
+            grid=(width,),
+            in_specs=[smem, head_rows, rate_rows, natural, natural, whole, whole]
+            + [anywhere] * held,
+            out_specs=[head_rows, turned, turned, inner0, inner0] + [state0] * levels,
+            out_shape=[row_shape, turned_shape, turned_shape, inner_shape, inner_shape]
+            + [jax.ShapeDtypeStruct((width * wide, dim), F32)] * levels,
+            input_output_aliases={7 + k: k for k in range(held)},
+            compiler_params=params,
+            name="states",
+            cost_estimate=pl.CostEstimate(flops=2 * 10**8 * width,
+                                          bytes_accessed=3 * 10**6 * width, transcendentals=0),
+        )(flags, steps, rates, x, g, bmap, cmap, *shared)
+        shared, fresh, read, payloads = results[:3], results[3], results[4], results[5:]
+        received = [lax.ppermute(payloads[d.bit_length() - 1], "ctx", pairs[d])
+                    for d in range(1, n)]
+        states.append((fresh, read, received))
+    logs, xt, gt = shared
 
     gf_in, rowsum, colsum, skip, gin, gout = pl.pallas_call(
         partial(intra_kernel, size),
-        grid=grid,
-        in_specs=[head_rows, head_rows, natural, turned, turned, whole, whole],
-        out_specs=[turned, head_rows, head_rows, head_rows, whole, whole],
+        grid=(groups,),
+        in_specs=[head_rows0, head_rows0, natural0, turned0, turned0, whole, whole],
+        out_specs=[turned0, head_rows0, head_rows0, head_rows0, whole, whole],
         out_shape=[jax.ShapeDtypeStruct((heads * size, length), F32), row_shape, row_shape,
                    row_shape, map_shape, map_shape],
         scratch_shapes=[pltpu.VMEM((blocks, Q, Q), F32)] * 2,
@@ -307,25 +371,47 @@
     leave = jnp.exp(jnp.where((others > me)[:, None], by_place, 0.0).sum(0))
     weights = jnp.stack([fore.at[0].set(enter), aft.at[0].set(leave)])
 
-    gf, gsteps, gin, gout, rate_part, skip_part = pl.pallas_call(
-        partial(finish_kernel, size, n - 1),
-        grid=grid,
-        in_specs=[smem, smem, head_rows, rate_rows, head_rows, head_rows, head_rows, head_rows,
-                  turned, turned, turned, whole, whole, whole, whole, state, state, inner, inner]
-        + [state] * (n - 1),
-        out_specs=[natural, head_rows, whole, whole, rate_rows, rate_rows],
-        out_shape=[jax.ShapeDtypeStruct((length, heads * size), BF16), row_shape, map_shape,
-                   map_shape, one_shape, one_shape],
-        scratch_shapes=[pltpu.VMEM((dim, length), F32)] * 2,
-        compiler_params=params,
-        name="finish",
-        cost_estimate=pl.CostEstimate(flops=2 * 10**9, bytes_accessed=30 * 10**6,
-                                      transcendentals=0),
-    )(weights, skip_gain, steps, rates, logs, rowsum, colsum, skip, xt, gt, gf_in, bmap, cmap,
-      gin, gout, state_first[0].reshape(heads * size, dim), state_last[0].reshape(heads * size, dim),
-      fresh, read, *received)
-    sums = lax.psum(jnp.concatenate([rate_part[:, 0], skip_part[:, 0]]), ("ctx", "seq"))
-    return (gf[None], gsteps[None], gin[None], gout[None], sums[:heads], sums[heads:])
+    grads, rate_parts, skip_parts = (), [], []
+    for (base, width), (fresh, read, received) in zip(chunks, states):
+        head_rows, rate_rows, natural, turned, state, inner = specs(base)
+        held = len(grads)
+        one_shape = jax.ShapeDtypeStruct((width * G, 1), F32)
+        *grads, gin, gout, rate_part, skip_part = pl.pallas_call(
+            partial(finish_kernel, size, n - 1, base, held),
+            grid=(width,),
+            in_specs=[smem, smem, head_rows, rate_rows, head_rows, head_rows, head_rows,
+                      head_rows, turned, turned, turned, whole, whole, whole, whole, state, state,
+                      inner0, inner0] + [state0] * (n - 1) + [anywhere] * held,
+            out_specs=[natural, head_rows, whole, whole, rate_rows0, rate_rows0],
+            out_shape=[jax.ShapeDtypeStruct((length, heads * size), BF16), row_shape, map_shape,
+                       map_shape, one_shape, one_shape],
+            scratch_shapes=[pltpu.VMEM((dim, length), F32)] * 2,
+            input_output_aliases={18 + n + k: k for k in range(held)},
+            compiler_params=params,
+            name="finish",
+            cost_estimate=pl.CostEstimate(flops=4 * 10**8 * width,
+                                          bytes_accessed=6 * 10**6 * width, transcendentals=0),
+        )(weights, skip_gain, steps, rates, logs, rowsum, colsum, skip, xt, gt, gf_in, bmap, cmap,
+          gin, gout, first, last, fresh, read, *received, *grads)
+        rate_parts.append(rate_part)
+        skip_parts.append(skip_part)
+    gf, gsteps = grads
+
+    lanes = -(-heads // 128) * 128
+    vmem = pl.BlockSpec(memory_space=pltpu.VMEM)
+    dma = pltpu.SemaphoreType.DMA
+    totals = pl.pallas_call(
+        partial(sums_kernel, n, m, len(chunks)),
+        in_specs=[vmem] * (2 * len(chunks)),
+        out_specs=vmem,
+        out_shape=jax.ShapeDtypeStruct((2, heads), F32),
+        scratch_shapes=[pltpu.VMEM((8, lanes), F32), pltpu.VMEM((n, 8, lanes), F32),
+                        pltpu.VMEM((m, 8, lanes), F32), dma((n,)), dma((n,)), dma((m,)),
+                        dma((m,))],
+        compiler_params=pltpu.CompilerParams(collective_id=0, has_side_effects=True),
+        name="sums",
+    )(*rate_parts, *skip_parts)
+    return (gf[None], gsteps[None], gin[None], gout[None], totals[0], totals[1])
 
 
 def solution(mesh):

time: 137 us -> 108 us (0.79)
  blocking collectives: 39.6 us -> 0 us
  Pallas kernels: 52.8 us -> 64.1 us
    psum x1 -> x0, blocking collectives: 39.6 us -> none  [local(): lax.psum(jnp.concatenate([rate_part[:, 0], skip_part[:, 0]]), ('ctx', 'se...]
    pallas_call x3 -> x4, Pallas kernels: 52.8 us -> 64.1 us  [the longest x1 30 us: local(): pl.pallas_call(partial(intra_kernel, size), grid=(groups,), in_specs=[hea...]
    pallas_call x3 -> x0, other arithmetic: 1.8 us -> none  [the longest x2 1.68 us: local(): pl.pallas_call(partial(finish_kernel, size, n - 1), grid=grid, in_specs=[...]
  transfers between devices with their start and end apart: 6 -> 6, of which waited for: 1 -> 1; matrix products, arithmetic and copies ran while one was open for 2% -> 3% of each run, Pallas kernels for 22% -> 37%
where the time goes in v2:
time: 108 us
  Pallas kernels  64.1 us (59%)
  waiting for transfers between devices  27.7 us (26%)
  starting transfers between devices  8.15 us (8%)
  local copies, waits for them, and re-layouts  3.99 us (4%)
  other arithmetic  3.24 us (3%)
    pallas_call x1, Pallas kernels, local(): pl.pallas_call(partial(intra_kernel, size), grid=(groups,), in_specs=[hea...  30 us
    ppermute x3, waiting for transfers between devices, local(): lax.ppermute(payloads[d.bit_length() - 1], 'ctx', pairs[d])  27.7 us
    pallas_call x1, Pallas kernels, local(): pl.pallas_call(partial(finish_kernel, size, n - 1, base, held), grid=(wid...  13.1 us
    pallas_call x1, Pallas kernels, local(): pl.pallas_call(partial(sums_kernel, n, m, len(chunks)), in_specs=[vmem] *...  11.3 us
    pallas_call x1, Pallas kernels, local(): pl.pallas_call(partial(states_kernel, size, held), grid=(width,), in_spec...  9.53 us
    ppermute x3, starting transfers between devices, local(): sums = [lax.ppermute(esum, 'ctx', pairs[d]) for d in range(1, n)]  4.47 us
    ppermute x3, starting transfers between devices, local(): lax.ppermute(payloads[d.bit_length() - 1], 'ctx', pairs[d])  3.69 us
  transfers between devices with their start and end apart: 6, of which 1 were waited for; matrix products, arithmetic and copies ran while one was open for 3% of the time, Pallas kernels for 37%

profile of v2, /device:TPU:0, one launch (start us, length us, event | category | flops | bytes accessed | tf_op | source)
XLA Modules:
  0.0 107.9 jit_solution(10540420386125164014)
XLA Ops:
  0.6 1.0 reduce_sum.45
  1.6 0.7 fusion.6
  2.3 3.9 %collective-permute-start.2 = (f32[40,1]{0,1:T(1,128)S(1)}, f32[40,1]{0,1:T(1,128)S(1)}, u32[]{:S(2)}, u32[]{:S(2)}) collective-permute-start(f32[40,1]{0,1:T(1,128)S(1)} %get-tuple-element.75), channel_id=1, source_target_pairs={{0,3},{1,2},{2,1},{3,0},{4,7},{5,6},{6,5},{7,4},{8,11},{9,10},{10,... | collective-permute-start | bytes 488 | tf_op jit(solution)/shard_map/ppermute | solution.py:320
  6.2 0.5 collective-permute-start.1
  6.7 0.1 collective-permute-start
  6.8 0.5 shift-right-arithmetic_and_fusion.flags
  7.3 0.7 copy.18.rates
  8.0 9.5 %states.1 = (f32[40,512]{1,0:T(8,128)}, bf16[2560,512]{1,0:T(8,128)(2,1)}, bf16[2560,512]{1,0:T(8,128)(2,1)}, f32[1,2560,128]{2,1,0:T(8,128)}, f32[1,2560,128]{2...) custom-call(s32[2]{0:T(128)} %shift-right-arithmetic_and_fusion.flags, f32[40,512]{1,0:T(8,128)} %bitcast.37, ...), custom_call_target="tpu_custom_call" | custom-call | flops 1000000000 | bytes 15000000 | tf_op jit(solution)/shard_map/states/pallas_call | solution.py:327
  17.5 3.0 %collective-permute-start.5 = (f32[2560,128]{1,0:T(8,128)}, f32[2560,128]{1,0:T(8,128)S(1)}, u32[]{:S(2)}, u32[]{:S(2)}) collective-permute-start(f32[2560,128]{1,0:T(8,128)} %get-tuple-element.61), channel_id=1, source_target_pairs={{0,3},{1,2},{2,1},{3,0},{4,7},{5,6},{6,5},{7,4},{8,11},{9,10},{10,... | collective-permute-start | bytes 3932168 | tf_op jit(solution)/shard_map/ppermute | solution.py:342
  20.5 0.5 collective-permute-start.4
  21.0 0.1 fusion.1
  21.1 30.0 %intra.1 = (f32[2560,512]{1,0:T(8,128)}, f32[40,512]{1,0:T(8,128)}, f32[40,512]{1,0:T(8,128)}, f32[40,512]{1,0:T(8,128)}, f32[512,128]{1,0:T(8,128)}, /*index=5*/f32[512,128]{1,0:T(8,128)}) custom-call(f32[40,512]{1,0:T(8,128)} %bitcast.38, f32[40,512]{1,0:T(8,128)} %get-tuple-element.49.logs, bf16[512,2560]{1,0:T(8,128)(2,1)} %bitcast.36, ...), custom_call_target="tpu_custom_call" | custom-call | flops 20000000000 | bytes 16000000 | tf_op jit(solution)/shard_map/intra/pallas_call | solution.py:347
  51.2 0.0 collective-permute-done.2
  51.2 0.2 collective-permute-start.3
  51.4 0.0 collective-permute-done.1
  51.4 0.0 collective-permute-done
  51.4 0.6 gather_fusion
  52.0 0.1 select_reduce_fusion.3
  52.1 0.1 select_reduce_fusion.1
  52.2 0.1 bitcast_select_fusion.1
  52.3 0.1 bitcast_select_fusion
  52.4 0.6 pad_maximum_fusion.weights
  53.0 27.7 %collective-permute-done.3.rest_0_ = f32[2560,128]{1,0:T(8,128)} collective-permute-done((f32[2560,128]{1,0:T(8,128)}, f32[2560,128]{1,0:T(8,128)}, u32[]{:S(2)}, u32[]{:S(2)}) %collective-permute-start.3) | collective-permute-done | bytes 1310752 | tf_op jit(solution)/shard_map/ppermute | solution.py:342
  80.7 0.0 collective-permute-done.5.rest_2_
  80.7 0.0 copy-start
  80.7 0.0 collective-permute-done.4.rest_1_
  80.7 0.0 copy-start.1
  80.7 1.1 copy-done
  81.8 0.4 copy-done.1
  82.1 13.1 %finish.1 = (bf16[512,2560]{1,0:T(8,128)(2,1)}, f32[40,512]{1,0:T(8,128)}, f32[512,128]{1,0:T(8,128)}, f32[512,128]{1,0:T(8,128)}, f32[40,1]{1,0:T(8,128)}, /*index=5*/f32[40,1]{1,0:T(8,128)}) custom-call(f32[2,4,40]{2,1,0:T(4,128)} %pad_maximum_fusion.weights, f32[40]{0:T(128)} %gains.1, f32[40,512]{1,0:T(8,128)} %bitcast.39, f32[40,1]{1,0:T(8,128)} %copy.18.rates, ...), custom_call_target="tpu_custom_call" | custom-call | flops 2000000000 | bytes 30000000 | tf_op jit(solution)/shard_map/finish/pallas_call | solution.py:379
  95.3 11.3 %sums.1 = f32[2,40]{1,0:T(2,128)} custom-call(f32[40,1]{1,0:T(8,128)} %get-tuple-element.66.refs_0_, f32[40,1]{1,0:T(8,128)} %get-tuple-element.67.refs_1_), custom_call_target="tpu_custom_call" | custom-call | tf_op jit(solution)/shard_map/sums/pallas_call | solution.py:403
  106.6 1.2 %slice_bitcast_fusion = (f32[40]{0:T(128)}, f32[40]{0:T(128)}) fusion(f32[2,40]{1,0:T(2,128)} %sums.1), kind=kLoop, calls=%fused_computation.16 | loop fusion | bytes 640 | tf_op jit(solution)/shard_map/squeeze | solution.py:414
  (11 shorter events, 0.1 us)
Async XLA Ops:
  2.3 48.9 %collective-permute-start.2 = (f32[40,1]{0,1:T(1,128)S(1)}, f32[40,1]{0,1:T(1,128)S(1)}, u32[]{:S(2)}, u32[]{:S(2)}) collective-permute-start(f32[40,1]{0,1:T(1,128)S(1)} %get-tuple-element.75), channel_id=1, source_target_pairs={{0,3},{1,2},{2,1},{3,0},{4,7},{5,6},{6,5},{7,4},{8,11},{9,10},{10,... | collective-permute-start | bytes 488 | tf_op jit(solution)/shard_map/ppermute | solution.py:320
  6.2 45.2 %collective-permute-start.1 = (f32[40,1]{0,1:T(1,128)S(1)}, f32[40,1]{0,1:T(1,128)S(1)}, u32[]{:S(2)}, u32[]{:S(2)}) collective-permute-start(f32[40,1]{0,1:T(1,128)S(1)} %get-tuple-element.75), channel_id=1, source_target_pairs={{0,2},{1,3},{2,0},{3,1},{4,6},{5,7},{6,4},{7,5},{8,10},{9,11},{10,... | collective-permute-start | bytes 488 | tf_op jit(solution)/shard_map/ppermute | solution.py:320
  6.7 44.7 %collective-permute-start = (f32[40,1]{0,1:T(1,128)S(1)}, f32[40,1]{0,1:T(1,128)S(1)}, u32[]{:S(2)}, u32[]{:S(2)}) collective-permute-start(f32[40,1]{0,1:T(1,128)S(1)} %get-tuple-element.75), channel_id=1, source_target_pairs={{0,1},{1,0},{2,3},{3,2},{4,5},{5,4},{6,7},{7,6},{8,9},{9,8},{10,11... | collective-permute-start | bytes 488 | tf_op jit(solution)/shard_map/ppermute | solution.py:320
  17.5 63.2 %collective-permute-start.5 = (f32[2560,128]{1,0:T(8,128)}, f32[2560,128]{1,0:T(8,128)S(1)}, u32[]{:S(2)}, u32[]{:S(2)}) collective-permute-start(f32[2560,128]{1,0:T(8,128)} %get-tuple-element.61), channel_id=1, source_target_pairs={{0,3},{1,2},{2,1},{3,0},{4,7},{5,6},{6,5},{7,4},{8,11},{9,10},{10,... | collective-permute-start | bytes 3932168 | tf_op jit(solution)/shard_map/ppermute | solution.py:342
  20.5 60.2 %collective-permute-start.4 = (f32[2560,128]{1,0:T(8,128)}, f32[2560,128]{1,0:T(8,128)S(1)}, u32[]{:S(2)}, u32[]{:S(2)}) collective-permute-start(f32[2560,128]{1,0:T(8,128)} %get-tuple-element.61), channel_id=1, source_target_pairs={{0,2},{1,3},{2,0},{3,1},{4,6},{5,7},{6,4},{7,5},{8,10},{9,11},{10,... | collective-permute-start | bytes 3932168 | tf_op jit(solution)/shard_map/ppermute | solution.py:342
  51.2 29.5 %collective-permute-start.3 = (f32[2560,128]{1,0:T(8,128)}, f32[2560,128]{1,0:T(8,128)}, u32[]{:S(2)}, u32[]{:S(2)}) collective-permute-start(f32[2560,128]{1,0:T(8,128)} %get-tuple-element.60), channel_id=1, source_target_pairs={{0,1},{1,0},{2,3},{3,2},{4,5},{5,4},{6,7},{7,6},{8,9},{9,8},{10,11... | collective-permute-start | bytes 3932168 | tf_op jit(solution)/shard_map/ppermute | solution.py:342
  80.7 1.1 copy-start
  80.7 1.4 %copy-start.1 = (f32[2560,128]{1,0:T(8,128)}, f32[2560,128]{1,0:T(8,128)S(1)}, u32[]{:S(2)}) copy-start(f32[2560,128]{1,0:T(8,128)S(1)} %collective-permute-done.4.rest_1_) | copy-start | bytes 3932164

commit v3 on v2

--- a/solution.py
+++ b/solution.py
@@ -30,9 +30,59 @@
     return (row <= col if kind == "prefix" else row >= col).astype(F32)
 
 
-def states_kernel(size, held, flags, steps, rates, x, g, bmap, cmap, *rest):
-    ls_out, xt_out, gt_out, fresh_out, read_out = rest[held : held + 5]
-    payloads = rest[held + 5 :]
+def partner(place, distance):
+    other = place
+    for k in range(distance.bit_length()):
+        if distance >> k & 1:
+            other = other + (1 - 2 * (place // 2**k % 2)) * 2**k
+    return other
+
+
+def local_kernel(size, n, steps, rates, x, g, bmap, cmap, *refs):
+    ls_out, xt_out, gt_out, fresh_out, read_out = refs[:5]
+    gf_out, rowsum, colsum, skip, gin, gout = refs[5:11]
+    received = refs[11 : 10 + n]
+    scores, total, logs, xts, gts, sent, send_sem, recv_sem = refs[10 + n :]
+    i = pl.program_id(0)
+    groups = pl.num_programs(0) // 2
+    me = lax.axis_index("ctx")
+
+    def copy(d, group):
+        return pltpu.make_async_remote_copy(
+            src_ref=sent.at[group, d.bit_length() - 1], dst_ref=received[d - 1].at[group],
+            send_sem=send_sem.at[d - 1, group], recv_sem=recv_sem.at[d - 1, group],
+            device_id={"ctx": partner(me, d)}, device_id_type=pl.DeviceIdType.MESH)
+
+    @pl.when(i == 0)
+    def _():
+        barrier = pltpu.get_barrier_semaphore()
+        for d in range(1, n):
+            pl.semaphore_signal(barrier, inc=1, device_id={"ctx": partner(me, d)},
+                                device_id_type=pl.DeviceIdType.MESH)
+        pl.semaphore_wait(barrier, n - 1)
+
+    @pl.when(i < groups)
+    def _():
+        states_step(size, n, me, steps, rates, x, g, bmap, cmap, ls_out, xt_out, gt_out,
+                    fresh_out, read_out, logs.at[i], xts.at[i], gts.at[i], sent.at[i])
+        for d in range(1, n):
+            copy(d, i).start()
+
+    @pl.when(i >= groups)
+    def _():
+        k = i - groups
+        intra_step(size, k, groups, steps, logs.at[k], g, xts.at[k], gts.at[k], bmap, cmap,
+                   gf_out, rowsum, colsum, skip, gin, gout, scores, total)
+
+    @pl.when(i == 2 * groups - 1)
+    def _():
+        for group in range(sent.shape[0]):
+            for d in range(1, n):
+                copy(d, group).wait()
+
+
+def states_step(size, n, me, steps, rates, x, g, bmap, cmap, ls_out, xt_out, gt_out, fresh_out,
+                read_out, logs_held, xt_held, gt_held, sent):
     blocks = steps.shape[1] // Q
     prefix = tri("prefix")
     fresh, read, ends = [], [], []
@@ -41,6 +91,7 @@
         step = steps[:, cols]
         logs = exact_dot(step * rates[...], prefix)
         ls_out[:, cols] = logs
+        logs_held[:, cols] = logs
         end = logs[:, Q - 1 :]
         scaled = jnp.exp(end - logs) * step
         grown = jnp.exp(logs)
@@ -48,6 +99,8 @@
         gt = g[cols, :].T
         xt_out[:, cols] = xt
         gt_out[:, cols] = gt
+        xt_held[:, cols] = xt
+        gt_held[:, cols] = gt
         xs, gs = [], []
         for h in range(G):
             rows = slice(h * size, (h + 1) * size)
@@ -67,13 +120,17 @@
             state = jnp.exp(ends[c][h : h + 1]) * state + fresh[c][rows]
             back = blocks - 1 - c
             cot = jnp.exp(ends[back][h : h + 1]) * cot + read[back][rows]
-        for k, payload in enumerate(payloads):
-            payload[rows, :] = jnp.where(flags[k] == 0, state, cot)
-
-
-def intra_kernel(size, steps, logs, g, xt, gt, bmap, cmap, gf_out, rowsum, colsum, skip,
-                 gin, gout, scores, total):
-    i = pl.program_id(0)
+        for k in range(n.bit_length() - 1):
+            sent[k, rows, :] = jnp.where(me // 2**k % 2 == 0, state, cot)
+    decay = ends[0]
+    for c in range(1, blocks):
+        decay = decay + ends[c]
+    for k in range(n.bit_length() - 1):
+        sent[k, G * size :, :] = jnp.broadcast_to(decay, (G, sent.shape[2]))
+
+
+def intra_step(size, i, groups, steps, logs, g, xt, gt, bmap, cmap, gf_out, rowsum, colsum, skip,
+               gin, gout, scores, total):
     blocks = steps.shape[1] // Q
     half = Q // 2
 
@@ -140,7 +197,7 @@
         rowsum[:, cols] = jnp.concatenate(sums, 1).T
         skip[:, cols] = jnp.concatenate(skips, 0)
 
-    @pl.when(i == pl.num_programs(0) - 1)
+    @pl.when(i == groups - 1)
     def _():
         for c in range(blocks):
             cols = slice(c * Q, (c + 1) * Q)
@@ -149,10 +206,10 @@
             gout[cols, :] = fdot(grads, bmap[cols, :])
 
 
-def finish_kernel(size, count, base, held, weights, gains, steps, rates, logs, rowsum, colsum, skip, xt, gt,
+def finish_kernel(size, count, weights, gains, steps, rates, logs, rowsum, colsum, skip, xt, gt,
                   gf_in, bmap, cmap, gin, gout, first, last, fresh, read, *rest):
     received = rest[:count]
-    gf, gsteps, gin_all, gout_all, rate_part, skip_part, tin, tout = rest[count + held :]
+    gf, gsteps, gin_all, gout_all, rate_part, skip_part, tin, tout = rest[count:]
     i = pl.program_id(0)
     blocks = steps.shape[1] // Q
     suffix = tri("suffix")
@@ -166,12 +223,12 @@
     entering = [[None] * G for _ in range(blocks)]
     leaving = [[None] * G for _ in range(blocks)]
     for h in range(G):
-        head = (base + i) * G + h
+        head = i * G + h
         rows = slice(h * size, (h + 1) * size)
         state = weights[0, 0, head] * first[rows].astype(F32)
         cot = weights[1, 0, head] * last[rows].astype(F32)
         for d in range(count):
-            value = received[d][rows]
+            value = received[d][0, rows]
             state = state + weights[0, d + 1, head] * value
             cot = cot + weights[1, d + 1, head] * value
         entering[0][h] = state
@@ -204,7 +261,7 @@
             rdots.append(jnp.sum(gh * out_t[rows], axis=0, keepdims=True))
             idots.append(jnp.sum(xh * in_t[rows], axis=0, keepdims=True))
             prods.append(jnp.sum(leaving[c][h] * entering[c][h], axis=0, keepdims=True))
-            grad = gf_in[rows, cols] + sc * in_t[rows] + gains[(base + i) * G + h] * gh
+            grad = gf_in[rows, cols] + sc * in_t[rows] + gains[i * G + h] * gh
             gf[cols, rows] = grad.T.astype(BF16)
         tin[:, cols] += lax.dot_general(lb, jnp.concatenate(xs, 0), TN, preferred_element_type=F32)
         tout[:, cols] += lax.dot_general(eb, jnp.concatenate(gs, 0), TN, preferred_element_type=F32)
@@ -291,75 +348,64 @@
     n, m = lax.axis_size("ctx"), lax.axis_size("seq")
     me = lax.axis_index("ctx")
     levels = n.bit_length() - 1
-    flags = (me >> jnp.arange(max(levels, 1))) & 1
     wide = G * size
     groups = heads // G
-    chunks = [(0, groups)]
     params = pltpu.CompilerParams(vmem_limit_bytes=56 * 1024 * 1024)
     smem = pl.BlockSpec(memory_space=pltpu.SMEM)
     anywhere = pl.BlockSpec(memory_space=pl.ANY)
     whole = pl.BlockSpec((length, dim), lambda i: (0, 0))
 
-    def specs(base):
+    def specs():
         return (
-            pl.BlockSpec((G, length), lambda i: (base + i, 0)),
-            pl.BlockSpec((G, 1), lambda i: (base + i, 0)),
-            pl.BlockSpec((length, wide), lambda i: (0, base + i)),
-            pl.BlockSpec((wide, length), lambda i: (base + i, 0)),
-            pl.BlockSpec((wide, dim), lambda i: (base + i, 0)),
-            pl.BlockSpec((blocks - 1, wide, dim), lambda i: (0, base + i, 0)),
+            pl.BlockSpec((G, length), lambda i: (i, 0)),
+            pl.BlockSpec((G, 1), lambda i: (i, 0)),
+            pl.BlockSpec((length, wide), lambda i: (0, i)),
+            pl.BlockSpec((wide, length), lambda i: (i, 0)),
+            pl.BlockSpec((wide, dim), lambda i: (i, 0)),
+            pl.BlockSpec((blocks - 1, wide, dim), lambda i: (0, i, 0)),
         )
 
-    head_rows0, rate_rows0, natural0, turned0, state0, inner0 = specs(0)
+    head_rows, rate_rows, natural, turned, state, inner = specs()
     row_shape = jax.ShapeDtypeStruct((heads, length), F32)
     map_shape = jax.ShapeDtypeStruct((length, dim), F32)
     turned_shape = jax.ShapeDtypeStruct((heads * size, length), BF16)
 
-    esum = jnp.sum(steps, axis=1, keepdims=True) * rates
-    pairs = [[(i, i ^ d) for i in range(n)] for d in range(n)]
-    sums = [lax.ppermute(esum, "ctx", pairs[d]) for d in range(1, n)]
-
-    shared, states = (), []
-    for base, width in chunks:
-        head_rows, rate_rows, natural, turned, state, inner = specs(base)
-        held = len(shared)
-        inner_shape = jax.ShapeDtypeStruct((blocks - 1, width * wide, dim), F32)
-        *shared, fresh, read = results = pl.pallas_call(
-            partial(states_kernel, size, held),
-            grid=(width,),
-            in_specs=[smem, head_rows, rate_rows, natural, natural, whole, whole]
-            + [anywhere] * held,
-            out_specs=[head_rows, turned, turned, inner0, inner0] + [state0] * levels,
-            out_shape=[row_shape, turned_shape, turned_shape, inner_shape, inner_shape]
-            + [jax.ShapeDtypeStruct((width * wide, dim), F32)] * levels,
-            input_output_aliases={7 + k: k for k in range(held)},
-            compiler_params=params,
-            name="states",
-            cost_estimate=pl.CostEstimate(flops=2 * 10**8 * width,
-                                          bytes_accessed=3 * 10**6 * width, transcendentals=0),
-        )(flags, steps, rates, x, g, bmap, cmap, *shared)
-        shared, fresh, read, payloads = results[:3], results[3], results[4], results[5:]
-        received = [lax.ppermute(payloads[d.bit_length() - 1], "ctx", pairs[d])
-                    for d in range(1, n)]
-        states.append((fresh, read, received))
-    logs, xt, gt = shared
-
-    gf_in, rowsum, colsum, skip, gin, gout = pl.pallas_call(
-        partial(intra_kernel, size),
-        grid=(groups,),
-        in_specs=[head_rows0, head_rows0, natural0, turned0, turned0, whole, whole],
-        out_specs=[turned0, head_rows0, head_rows0, head_rows0, whole, whole],
-        out_shape=[jax.ShapeDtypeStruct((heads * size, length), F32), row_shape, row_shape,
-                   row_shape, map_shape, map_shape],
-        scratch_shapes=[pltpu.VMEM((blocks, Q, Q), F32)] * 2,
-        compiler_params=params,
-        name="intra",
-        cost_estimate=pl.CostEstimate(flops=2 * 10**10, bytes_accessed=16 * 10**6,
+    both = pl.BlockSpec((G, length), lambda i: (lax.rem(i, groups), 0))
+    both_rates = pl.BlockSpec((G, 1), lambda i: (lax.rem(i, groups), 0))
+    both_natural = pl.BlockSpec((length, wide), lambda i: (0, lax.rem(i, groups)))
+    early_natural = pl.BlockSpec((length, wide), lambda i: (0, jnp.minimum(i, groups - 1)))
+    early_rows = pl.BlockSpec((G, length), lambda i: (jnp.minimum(i, groups - 1), 0))
+    early_turned = pl.BlockSpec((wide, length), lambda i: (jnp.minimum(i, groups - 1), 0))
+    early_inner = pl.BlockSpec((blocks - 1, wide, dim), lambda i: (0, jnp.minimum(i, groups - 1), 0))
+    late_turned = pl.BlockSpec((wide, length), lambda i: (jnp.maximum(i - groups, 0), 0))
+    late_rows = pl.BlockSpec((G, length), lambda i: (jnp.maximum(i - groups, 0), 0))
+    inner_shape = jax.ShapeDtypeStruct((blocks - 1, heads * size, dim), F32)
+    message = jax.ShapeDtypeStruct((groups, wide + G, dim), F32)
+    (logs, xt, gt, fresh, read, gf_in, rowsum, colsum, skip, gin, gout, *received) = pl.pallas_call(
+        partial(local_kernel, size, n),
+        grid=(2 * groups,),
+        in_specs=[both, both_rates, early_natural, both_natural, whole, whole],
+        out_specs=[early_rows, early_turned, early_turned, early_inner, early_inner,
+                   late_turned, late_rows, late_rows, late_rows, whole, whole]
+        + [anywhere] * (n - 1),
+        out_shape=[row_shape, turned_shape, turned_shape, inner_shape, inner_shape,
+                   jax.ShapeDtypeStruct((heads * size, length), F32), row_shape, row_shape,
+                   row_shape, map_shape, map_shape] + [message] * (n - 1),
+        scratch_shapes=[pltpu.VMEM((blocks, Q, Q), F32)] * 2
+        + [pltpu.VMEM((groups, G, length), F32)]
+        + [pltpu.VMEM((groups, wide, length), BF16)] * 2
+        + [pltpu.VMEM((groups, levels, wide + G, dim), F32),
+           pltpu.SemaphoreType.DMA((n - 1, groups)), pltpu.SemaphoreType.DMA((n - 1, groups))],
+        compiler_params=pltpu.CompilerParams(vmem_limit_bytes=56 * 1024 * 1024, collective_id=1,
+                                             has_side_effects=True),
+        name="local_grads",
+        cost_estimate=pl.CostEstimate(flops=2 * 10**10, bytes_accessed=30 * 10**6,
                                       transcendentals=0),
-    )(steps, logs, g, xt, gt, bmap, cmap)
+    )(steps, rates, x, g, bmap, cmap)
 
     others = jnp.arange(n)
-    by_distance = jnp.stack([esum[:, 0]] + [s[:, 0] for s in sums])
+    esum = logs[:, Q - 1 :: Q].sum(1)
+    by_distance = jnp.stack([esum] + [r[:, wide:, 0].reshape(heads) for r in received])
     by_place = by_distance[others ^ me]
     source = (me ^ others)[:, None]
     between = others[None, :]
@@ -371,38 +417,31 @@
     leave = jnp.exp(jnp.where((others > me)[:, None], by_place, 0.0).sum(0))
     weights = jnp.stack([fore.at[0].set(enter), aft.at[0].set(leave)])
 
-    grads, rate_parts, skip_parts = (), [], []
-    for (base, width), (fresh, read, received) in zip(chunks, states):
-        head_rows, rate_rows, natural, turned, state, inner = specs(base)
-        held = len(grads)
-        one_shape = jax.ShapeDtypeStruct((width * G, 1), F32)
-        *grads, gin, gout, rate_part, skip_part = pl.pallas_call(
-            partial(finish_kernel, size, n - 1, base, held),
-            grid=(width,),
-            in_specs=[smem, smem, head_rows, rate_rows, head_rows, head_rows, head_rows,
-                      head_rows, turned, turned, turned, whole, whole, whole, whole, state, state,
-                      inner0, inner0] + [state0] * (n - 1) + [anywhere] * held,
-            out_specs=[natural, head_rows, whole, whole, rate_rows0, rate_rows0],
-            out_shape=[jax.ShapeDtypeStruct((length, heads * size), BF16), row_shape, map_shape,
-                       map_shape, one_shape, one_shape],
-            scratch_shapes=[pltpu.VMEM((dim, length), F32)] * 2,
-            input_output_aliases={18 + n + k: k for k in range(held)},
-            compiler_params=params,
-            name="finish",
-            cost_estimate=pl.CostEstimate(flops=4 * 10**8 * width,
-                                          bytes_accessed=6 * 10**6 * width, transcendentals=0),
-        )(weights, skip_gain, steps, rates, logs, rowsum, colsum, skip, xt, gt, gf_in, bmap, cmap,
-          gin, gout, first, last, fresh, read, *received, *grads)
-        rate_parts.append(rate_part)
-        skip_parts.append(skip_part)
-    gf, gsteps = grads
+    one_shape = jax.ShapeDtypeStruct((heads, 1), F32)
+    arrived = pl.BlockSpec((1, wide + G, dim), lambda i: (i, 0, 0))
+    gf, gsteps, gin, gout, rate_part, skip_part = pl.pallas_call(
+        partial(finish_kernel, size, n - 1),
+        grid=(groups,),
+        in_specs=[smem, smem, head_rows, rate_rows, head_rows, head_rows, head_rows,
+                  head_rows, turned, turned, turned, whole, whole, whole, whole, state, state,
+                  inner, inner] + [arrived] * (n - 1),
+        out_specs=[natural, head_rows, whole, whole, rate_rows, rate_rows],
+        out_shape=[jax.ShapeDtypeStruct((length, heads * size), BF16), row_shape, map_shape,
+                   map_shape, one_shape, one_shape],
+        scratch_shapes=[pltpu.VMEM((dim, length), F32)] * 2,
+        compiler_params=params,
+        name="finish",
+        cost_estimate=pl.CostEstimate(flops=2 * 10**9, bytes_accessed=30 * 10**6,
+                                      transcendentals=0),
+    )(weights, skip_gain, steps, rates, logs, rowsum, colsum, skip, xt, gt, gf_in, bmap, cmap,
+      gin, gout, first, last, fresh, read, *received)
 
     lanes = -(-heads // 128) * 128
     vmem = pl.BlockSpec(memory_space=pltpu.VMEM)
     dma = pltpu.SemaphoreType.DMA
     totals = pl.pallas_call(
-        partial(sums_kernel, n, m, len(chunks)),
-        in_specs=[vmem] * (2 * len(chunks)),
+        partial(sums_kernel, n, m, 1),
+        in_specs=[vmem] * 2,
         out_specs=vmem,
         out_shape=jax.ShapeDtypeStruct((2, heads), F32),
         scratch_shapes=[pltpu.VMEM((8, lanes), F32), pltpu.VMEM((n, 8, lanes), F32),
@@ -410,7 +449,7 @@
                         dma((m,))],
         compiler_params=pltpu.CompilerParams(collective_id=0, has_side_effects=True),
         name="sums",
-    )(*rate_parts, *skip_parts)
+    )(rate_part, skip_part)
     return (gf[None], gsteps[None], gin[None], gout[None], totals[0], totals[1])
 
 

time: 108 us -> 99.7 us (0.923)
  waiting for transfers between devices: 27.7 us -> 0 us
  Pallas kernels: 64.1 us -> 91.2 us
  starting transfers between devices: 8.15 us -> 0 us
  other arithmetic: 3.24 us -> 1.82 us
  local copies, waits for them, and re-layouts: 3.99 us -> 5.4 us
    ppermute x6 -> x0, waiting for transfers between devices: 27.7 us -> none  [the longest x3 27.7 us: local(): lax.ppermute(payloads[d.bit_length() - 1], 'ctx', pairs[d])]
    pallas_call x4 -> x3, Pallas kernels: 64.1 us -> 91.2 us  [the longest x1 66.5 us: local(): pl.pallas_call(partial(local_kernel, size, n), grid=(2 * groups,), in_spe...]
    ppermute x6 -> x0, starting transfers between devices: 8.15 us -> none  [the longest x3 4.47 us: local(): sums = [lax.ppermute(esum, 'ctx', pairs[d]) for d in range(1, n)]]
    slice x0 -> x3, local copies, waits for them, and re-layouts: none -> 2.56 us  [the longest x2 1.64 us: local(): r[:, wide:, 0].reshape(heads)]
    unnamed x4 -> x0, local copies, waits for them, and re-layouts: 1.44 us -> none
  transfers between devices with their start and end apart: 6 -> 0, of which waited for: 1 -> 0; matrix products, arithmetic and copies ran while one was open for 3% -> 0% of each run, Pallas kernels for 37% -> 0%
where the time goes in v3:
time: 99.7 us; the launch traced here: 99.1 us
  Pallas kernels  91.2 us (91%)
  local copies, waits for them, and re-layouts  5.4 us (5%)
  other arithmetic  1.82 us (2%)
    pallas_call x1, Pallas kernels, local(): pl.pallas_call(partial(local_kernel, size, n), grid=(2 * groups,), in_spe...  66.5 us
    pallas_call x1, Pallas kernels, local(): pl.pallas_call(partial(finish_kernel, size, n - 1), grid=(groups,), in_sp...  13.2 us
    pallas_call x1, Pallas kernels, local(): pl.pallas_call(partial(sums_kernel, n, m, 1), in_specs=[vmem] * 2, out_sp...  11.5 us

profile of v3, /device:TPU:0, one launch (start us, length us, event | category | flops | bytes accessed | tf_op | source)
XLA Modules:
  0.0 99.1 jit_solution(17229087444462818959)
XLA Ops:
  0.6 0.7 negate_bitcast_fusion
  1.4 0.1 fusion.1
  1.4 0.7 copy.19.rates
  2.1 66.5 %local_grads.1 = (f32[40,512]{1,0:T(8,128)}, bf16[2560,512]{1,0:T(8,128)(2,1)}, bf16[2560,512]{1,0:T(8,128)(2,1)}, f32[1,2560,128]{2,1,0:T(8,128)}, f32[1,2560,1...) custom-call(f32[40,512]{1,0:T(8,128)} %bitcast.34, ...), custom_call_target="tpu_custom_call" | custom-call | flops 20000000000 | bytes 30000000 | tf_op jit(solution)/shard_map/local_grads/pallas_call | solution.py:384
  68.7 0.8 slice_reduce_fusion.2
  69.5 0.1 stack_reshape_squeeze.9
  69.5 0.8 slice_reduce_fusion
  70.4 0.1 stack_reshape_squeeze.11
  70.5 0.1 stack_reshape_squeeze.10
  70.5 0.9 slice.48
  71.5 0.1 reduce_sum.45
  71.6 0.6 gather_fusion
  72.1 0.1 select_reduce_fusion.3
  72.3 0.1 select_reduce_fusion.1
  72.4 0.1 bitcast_select_fusion.1
  72.5 0.1 bitcast_select_fusion
  72.6 0.6 pad_maximum_fusion.weights
  73.2 13.2 %finish.1 = (bf16[512,2560]{1,0:T(8,128)(2,1)}, f32[40,512]{1,0:T(8,128)}, f32[512,128]{1,0:T(8,128)}, f32[512,128]{1,0:T(8,128)}, f32[40,1]{1,0:T(8,128)}, /*index=5*/f32[40,1]{1,0:T(8,128)}) custom-call(f32[2,4,40]{2,1,0:T(4,128)} %pad_maximum_fusion.weights, f32[40]{0:T(128)} %gains.1, f32[40,512]{1,0:T(8,128)} %bitcast.35, f32[40,1]{1,0:T(8,128)} %copy.19.rates, ...), custom_call_target="tpu_custom_call" | custom-call | flops 2000000000 | bytes 30000000 | tf_op jit(solution)/shard_map/finish/pallas_call | solution.py:422
  86.4 11.5 %sums.1 = f32[2,40]{1,0:T(2,128)} custom-call(f32[40,1]{1,0:T(8,128)} %get-tuple-element.68.refs_0_, f32[40,1]{1,0:T(8,128)} %get-tuple-element.69.refs_1_), custom_call_target="tpu_custom_call" | custom-call | tf_op jit(solution)/shard_map/sums/pallas_call | solution.py:442
  97.8 1.3 %slice_bitcast_fusion = (f32[40]{0:T(128)}, f32[40]{0:T(128)}) fusion(f32[2,40]{1,0:T(2,128)} %sums.1), kind=kLoop, calls=%fused_computation.19 | loop fusion | bytes 640 | tf_op jit(solution)/shard_map/squeeze | solution.py:453
  (11 shorter events, 0.1 us)

commit v4 on v3

--- a/solution.py
+++ b/solution.py
@@ -41,15 +41,14 @@
 def local_kernel(size, n, steps, rates, x, g, bmap, cmap, *refs):
     ls_out, xt_out, gt_out, fresh_out, read_out = refs[:5]
     gf_out, rowsum, colsum, skip, gin, gout = refs[5:11]
-    received = refs[11 : 10 + n]
-    scores, total, logs, xts, gts, sent, send_sem, recv_sem = refs[10 + n :]
+    received, scores, total, logs, xts, gts, sent, send_sem, recv_sem = refs[11:]
     i = pl.program_id(0)
     groups = pl.num_programs(0) // 2
     me = lax.axis_index("ctx")
 
     def copy(d, group):
         return pltpu.make_async_remote_copy(
-            src_ref=sent.at[group, d.bit_length() - 1], dst_ref=received[d - 1].at[group],
+            src_ref=sent.at[group, d.bit_length() - 1], dst_ref=received.at[d - 1, group],
             send_sem=send_sem.at[d - 1, group], recv_sem=recv_sem.at[d - 1, group],
             device_id={"ctx": partner(me, d)}, device_id_type=pl.DeviceIdType.MESH)
 
@@ -228,7 +227,7 @@
         state = weights[0, 0, head] * first[rows].astype(F32)
         cot = weights[1, 0, head] * last[rows].astype(F32)
         for d in range(count):
-            value = received[d][0, rows]
+            value = received[d][0, 0, rows]
             state = state + weights[0, d + 1, head] * value
             cot = cot + weights[1, d + 1, head] * value
         entering[0][h] = state
@@ -380,17 +379,17 @@
     late_turned = pl.BlockSpec((wide, length), lambda i: (jnp.maximum(i - groups, 0), 0))
     late_rows = pl.BlockSpec((G, length), lambda i: (jnp.maximum(i - groups, 0), 0))
     inner_shape = jax.ShapeDtypeStruct((blocks - 1, heads * size, dim), F32)
-    message = jax.ShapeDtypeStruct((groups, wide + G, dim), F32)
-    (logs, xt, gt, fresh, read, gf_in, rowsum, colsum, skip, gin, gout, *received) = pl.pallas_call(
+    message = jax.ShapeDtypeStruct((n - 1, groups, wide + G, dim), F32)
+    (logs, xt, gt, fresh, read, gf_in, rowsum, colsum, skip, gin, gout, received) = pl.pallas_call(
         partial(local_kernel, size, n),
         grid=(2 * groups,),
         in_specs=[both, both_rates, early_natural, both_natural, whole, whole],
         out_specs=[early_rows, early_turned, early_turned, early_inner, early_inner,
                    late_turned, late_rows, late_rows, late_rows, whole, whole]
-        + [anywhere] * (n - 1),
+        + [anywhere],
         out_shape=[row_shape, turned_shape, turned_shape, inner_shape, inner_shape,
                    jax.ShapeDtypeStruct((heads * size, length), F32), row_shape, row_shape,
-                   row_shape, map_shape, map_shape] + [message] * (n - 1),
+                   row_shape, map_shape, map_shape, message],
         scratch_shapes=[pltpu.VMEM((blocks, Q, Q), F32)] * 2
         + [pltpu.VMEM((groups, G, length), F32)]
         + [pltpu.VMEM((groups, wide, length), BF16)] * 2
@@ -405,7 +404,7 @@
 
     others = jnp.arange(n)
     esum = logs[:, Q - 1 :: Q].sum(1)
-    by_distance = jnp.stack([esum] + [r[:, wide:, 0].reshape(heads) for r in received])
+    by_distance = jnp.concatenate([esum[None], received[:, :, wide:, 0].reshape(n - 1, heads)])
     by_place = by_distance[others ^ me]
     source = (me ^ others)[:, None]
     between = others[None, :]
@@ -418,13 +417,13 @@
     weights = jnp.stack([fore.at[0].set(enter), aft.at[0].set(leave)])
 
     one_shape = jax.ShapeDtypeStruct((heads, 1), F32)
-    arrived = pl.BlockSpec((1, wide + G, dim), lambda i: (i, 0, 0))
+    arrived = [pl.BlockSpec((1, 1, wide + G, dim), lambda i, d=d: (d, i, 0, 0)) for d in range(n - 1)]
     gf, gsteps, gin, gout, rate_part, skip_part = pl.pallas_call(
         partial(finish_kernel, size, n - 1),
         grid=(groups,),
         in_specs=[smem, smem, head_rows, rate_rows, head_rows, head_rows, head_rows,
                   head_rows, turned, turned, turned, whole, whole, whole, whole, state, state,
-                  inner, inner] + [arrived] * (n - 1),
+                  inner, inner] + arrived,
         out_specs=[natural, head_rows, whole, whole, rate_rows, rate_rows],
         out_shape=[jax.ShapeDtypeStruct((length, heads * size), BF16), row_shape, map_shape,
                    map_shape, one_shape, one_shape],
@@ -434,7 +433,7 @@
         cost_estimate=pl.CostEstimate(flops=2 * 10**9, bytes_accessed=30 * 10**6,
                                       transcendentals=0),
     )(weights, skip_gain, steps, rates, logs, rowsum, colsum, skip, xt, gt, gf_in, bmap, cmap,
-      gin, gout, first, last, fresh, read, *received)
+      gin, gout, first, last, fresh, read, *[received] * (n - 1))
 
     lanes = -(-heads // 128) * 128
     vmem = pl.BlockSpec(memory_space=pltpu.VMEM)

time: 99.7 us -> 98.7 us (0.990)
  no operation moved by 1% of the time
where the time goes in v4:
time: 98.7 us; the launch traced here: 98.2 us
  Pallas kernels  91.1 us (92%)
  local copies, waits for them, and re-layouts  4.52 us (5%)
  other arithmetic  1.83 us (2%)
    pallas_call x1, Pallas kernels, local(): pl.pallas_call(partial(local_kernel, size, n), grid=(2 * groups,), in_spe...  66.5 us
    pallas_call x1, Pallas kernels, local(): pl.pallas_call(partial(finish_kernel, size, n - 1), grid=(groups,), in_sp...  13.1 us
    pallas_call x1, Pallas kernels, local(): pl.pallas_call(partial(sums_kernel, n, m, 1), in_specs=[vmem] * 2, out_sp...  11.5 us

profile of v4, /device:TPU:0, one launch (start us, length us, event | category | flops | bytes accessed | tf_op | source)
XLA Modules:
  0.0 98.2 jit_solution(1730289877692002816)
XLA Ops:
  0.6 0.7 negate_bitcast_fusion
  1.4 0.1 fusion.1
  1.4 0.7 copy.19.rates
  2.1 66.5 %local_grads.1 = (f32[40,512]{1,0:T(8,128)}, bf16[2560,512]{1,0:T(8,128)(2,1)}, bf16[2560,512]{1,0:T(8,128)(2,1)}, f32[1,2560,128]{2,1,0:T(8,128)}, f32[1,2560,1...) custom-call(f32[40,512]{1,0:T(8,128)} %bitcast.34, ...), custom_call_target="tpu_custom_call" | custom-call | flops 20000000000 | bytes 30000000 | tf_op jit(solution)/shard_map/local_grads/pallas_call | solution.py:383
  68.6 0.9 slice_reduce_fusion
  69.6 0.1 reshape_squeeze.9
  69.6 0.9 slice.42
  70.6 0.1 reduce_sum.45
  70.7 0.6 gather_fusion
  71.2 0.1 select_reduce_fusion.3
  71.4 0.1 select_reduce_fusion.1
  71.5 0.1 bitcast_select_fusion.1
  71.6 0.1 bitcast_select_fusion
  71.7 0.6 pad_maximum_fusion.weights
  72.3 13.1 %finish.1 = (bf16[512,2560]{1,0:T(8,128)(2,1)}, f32[40,512]{1,0:T(8,128)}, f32[512,128]{1,0:T(8,128)}, f32[512,128]{1,0:T(8,128)}, f32[40,1]{1,0:T(8,128)}, /*index=5*/f32[40,1]{1,0:T(8,128)}) custom-call(f32[2,4,40]{2,1,0:T(4,128)} %pad_maximum_fusion.weights, f32[40]{0:T(128)} %gains.1, f32[40,512]{1,0:T(8,128)} %bitcast.35, f32[40,1]{1,0:T(8,128)} %copy.19.rates, ...), custom_call_target="tpu_custom_call" | custom-call | flops 2000000000 | bytes 30000000 | tf_op jit(solution)/shard_map/finish/pallas_call | solution.py:421
  85.4 11.5 %sums.1 = f32[2,40]{1,0:T(2,128)} custom-call(f32[40,1]{1,0:T(8,128)} %get-tuple-element.64.refs_0_, f32[40,1]{1,0:T(8,128)} %get-tuple-element.65.refs_1_), custom_call_target="tpu_custom_call" | custom-call | tf_op jit(solution)/shard_map/sums/pallas_call | solution.py:441
  96.9 1.3 %slice_bitcast_fusion = (f32[40]{0:T(128)}, f32[40]{0:T(128)}) fusion(f32[2,40]{1,0:T(2,128)} %sums.1), kind=kLoop, calls=%fused_computation.17 | loop fusion | bytes 640 | tf_op jit(solution)/shard_map/squeeze | solution.py:452
  (11 shorter events, 0.1 us)
